TPU v7x, 32 devices: a whole 2x2x4 slice. The times are simulated.
32 devices in a mesh: psg: 4 (over z), exp: 8 (over y, x, core).
Axes of the slice: x: 2, y: 2, z: 4, core: 2. Of those that a mesh axis runs over, the one named last changes fastest.
Arguments:
- hidden: bfloat16 [8, 4, 128, 2048], P('exp', 'psg')
- norm_gain: float32 [2048], replicated, may hold values from 0.5 to 2
- router: bfloat16 [2048, 8], replicated, may hold values from -0.125 to 0.125
- gate_proj: bfloat16 [8, 2048, 768], P('exp'), may hold values from -0.125 to 0.125
- up_proj: bfloat16 [8, 2048, 768], P('exp'), may hold values from -0.125 to 0.125
- down_proj: bfloat16 [8, 768, 2048], P('exp'), may hold values from -0.21875 to 0.21875
- final_gain: float32 [2048], replicated, may hold values from 0.5 to 2
- score_vector: bfloat16 [2048], replicated, may hold values from -0.125 to 0.125
- expert_ids: int32 [8, 4, 128, 8], P('exp', 'psg'), may hold values from 0 to 7, as said below
- grades: int32 [8, 4], P('exp'), may hold values from 0 to 4, as said below
- passage_ranks: int32 [8, 4], P('exp'), may hold values from 0 to 3, each once within a row
Outputs:
- loss: float32 [8], P('exp')
- scores: float32 [8, 4], P('exp', 'psg')
- grad_hidden: bfloat16 [8, 4, 128, 2048], P('exp', 'psg')
Inputs may be any that keep to these rules, and one draw needn't show every extreme that they name: `expert_ids`: each token names 8 different experts. Among the tokens of one device each expert is named at most 128 times, and one expert, the same on every device, is named exactly 128 times on every device. `grades`: every query has some passage of grade 4. `passage_ranks`: each rank appears once in each query.
All inputs are finite; a program needn't handle non-finite values.
Results may differ from a plain program's by a relative error of at most 0.0067.
Values may be sent and summed in bfloat16 or wider, within the bound.
No kernel may reach another device: no remote copies, remote signals or barrier semaphores. Data moves between devices by JAX's collectives and lax.ppermute only.
A program may use at most 128 MiB of HBM per device.

v0:
```python
import functools
import math

import jax
import jax.numpy as jnp
from jax import lax
from jax.experimental import pallas as pl
from jax.experimental.pallas import tpu as pltpu
from jax.sharding import PartitionSpec as P

epsilon = 1e-06
loss_scale = 256.0
highest = lax.Precision.HIGHEST


def rms_scale(values):
    return lax.rsqrt(jnp.mean(values * values, axis=-1, keepdims=True) + epsilon)


def head_score(pooled, final_gain, score_vector):
    scaled = pooled * rms_scale(pooled) * final_gain
    return jnp.dot(scaled, score_vector.astype(jnp.float32), precision=highest)


def rank_loss(scores, grades, passage_ranks):
    grade_value = grades.astype(jnp.float32)
    worth_gain = jnp.exp2(grade_value)
    discount = 1.0 / jnp.log2(2.0 + passage_ranks.astype(jnp.float32))
    better_than = grades[None, :] > grades[:, None]
    equal_grade = grades[None, :] == grades[:, None]
    position = jnp.arange(grades.shape[0], dtype=jnp.int32)
    earlier = position[None, :] < position[:, None]
    ideal_rank = jnp.sum(
        jnp.logical_or(better_than, jnp.logical_and(equal_grade, earlier)).astype(jnp.float32),
        axis=1,
    )
    ideal_gain = jnp.sum((worth_gain - 1.0) / jnp.log2(2.0 + ideal_rank))
    ordered = (grades[:, None] > grades[None, :]).astype(jnp.float32)
    swap_gain = (
        jnp.abs(
            (worth_gain[:, None] - worth_gain[None, :]) * (discount[:, None] - discount[None, :])
        )
        / ideal_gain
    )
    margin = scores[:, None] - scores[None, :]
    return jnp.sum(ordered * swap_gain * jax.nn.softplus(-margin))


def pick_gates(normed, router, picked_ids):
    expert_total = router.shape[1]
    logits = jnp.dot(normed, router, preferred_element_type=jnp.float32)
    onehot = (
        picked_ids[:, :, None] == jnp.arange(expert_total, dtype=jnp.int32)[None, None, :]
    ).astype(jnp.float32)
    chosen = jnp.einsum("nke,ne->nk", onehot, logits, precision=highest)
    weights = jnp.exp(chosen)
    return (weights / jnp.sum(weights, axis=1, keepdims=True), onehot)


def gate_parts(pre_gate):
    sigmoid_gate = jax.nn.sigmoid(pre_gate)
    return (pre_gate * sigmoid_gate, sigmoid_gate * (1.0 + pre_gate * (1.0 - sigmoid_gate)))


def norm_back(flat_rows, inverse, norm_gain, d_normed):
    scaled = d_normed * norm_gain
    return inverse * scaled - flat_rows * inverse * inverse * inverse * jnp.mean(
        flat_rows * scaled, axis=-1, keepdims=True
    )


def unpack_front(front_out, buffer_rows):
    pre_gate, pre_up, received = front_out
    hidden_units = pre_gate.shape[2]
    pre_gate = pre_gate.reshape(buffer_rows, hidden_units)
    pre_up = pre_up.reshape(buffer_rows, hidden_units)
    silu_gate, slope = gate_parts(pre_gate)
    activation = (silu_gate * pre_up).astype(jnp.bfloat16)
    return (pre_up, received, silu_gate, slope, activation)


def local(
    hidden,
    norm_gain,
    router,
    gate_proj,
    up_proj,
    down_proj,
    final_gain,
    score_vector,
    expert_ids,
    grades,
    passage_ranks,
):
    unused_query, local_passages, local_positions, model_width = hidden.shape
    top_count = expert_ids.shape[3]
    expert_count = lax.axis_size("exp")
    token_count = local_passages * local_positions
    slot_count = token_count * top_count
    capacity = min(token_count, 9 * token_count * top_count // (8 * expert_count))
    buffer_rows = expert_count * capacity
    flat_rows = hidden.reshape(token_count, model_width).astype(jnp.float32)
    inverse = rms_scale(flat_rows)
    normed = (flat_rows * inverse * norm_gain).astype(jnp.bfloat16)
    picked_ids = expert_ids.reshape(token_count, top_count)
    gate_values, onehot = pick_gates(normed, router, picked_ids)
    slot_hits = onehot.reshape(slot_count, expert_count).astype(jnp.int32)
    slot_rank = jnp.sum((jnp.cumsum(slot_hits, axis=0) - slot_hits) * slot_hits, axis=1)
    target = picked_ids.reshape(slot_count) * capacity + slot_rank
    source_token = jnp.arange(slot_count, dtype=jnp.int32) // top_count
    passage_onehot = (
        source_token[:, None] // local_positions
        == jnp.arange(local_passages, dtype=jnp.int32)[None, :]
    ).astype(jnp.float32)
    weighted = (passage_onehot * gate_values.reshape(slot_count, 1)).astype(jnp.bfloat16)
    send_rows = (
        jnp.zeros((buffer_rows, model_width), jnp.bfloat16).at[target].set(normed[source_token])
    )
    send_weights = jnp.zeros((buffer_rows, local_passages), jnp.bfloat16).at[target].set(weighted)
    outgoing = (
        send_rows.reshape(expert_count, capacity, model_width),
        send_weights.reshape(expert_count, capacity, local_passages),
    )
    gate_matrix = gate_proj[0]
    up_matrix = up_proj[0]
    down_matrix = down_proj[0]
    rows_in = lax.all_to_all(outgoing[0], "exp", split_axis=0, concat_axis=0, tiled=True)
    weights_in = lax.all_to_all(outgoing[1], "exp", split_axis=0, concat_axis=0, tiled=True)
    pre_gate = jnp.einsum("end,df->enf", rows_in, gate_matrix, preferred_element_type=jnp.float32)
    pre_up = jnp.einsum("end,df->enf", rows_in, up_matrix, preferred_element_type=jnp.float32)
    front_out = (pre_gate, pre_up, weights_in)
    pre_up, received, silu_gate, slope, activation = unpack_front(front_out, buffer_rows)
    hidden_units = activation.shape[1]
    passage_part = jnp.einsum(
        "scp,scf->spf",
        received,
        activation.reshape(expert_count, capacity, hidden_units),
        preferred_element_type=jnp.float32,
    )
    down_wide = down_matrix.astype(jnp.float32)
    expert_terms = jnp.einsum("spf,fd->spd", passage_part, down_wide, precision=highest)
    came_back = lax.all_to_all(expert_terms, "exp", split_axis=0, concat_axis=0, tiled=True)
    token_sums = jnp.sum(flat_rows.reshape(local_passages, local_positions, model_width), axis=1)
    pooled = (token_sums + jnp.sum(came_back, axis=0)) / local_positions
    first_row = lax.axis_index("psg") * local_passages
    own_score = head_score(pooled, final_gain, score_vector)
    every_score = lax.all_gather(own_score, "psg", axis=0, tiled=True)
    loss_value, loss_grad = jax.value_and_grad(rank_loss)(every_score, grades[0], passage_ranks[0])
    d_own = lax.dynamic_slice_in_dim(loss_grad, first_row, local_passages, 0) * loss_scale
    unused_score, head_back = jax.vjp(
        lambda values: head_score(values, final_gain, score_vector), pooled
    )
    d_vector = head_back(d_own)[0] / local_positions
    every_vector = lax.all_gather(d_vector[None], "exp", axis=0, tiled=True)
    near_table = jnp.einsum("spd,fd->spf", every_vector, down_wide, precision=highest)
    present = (received != 0).astype(jnp.float32)
    near_rows = jnp.einsum("scp,spf->scf", present, near_table, precision=highest).reshape(
        buffer_rows, hidden_units
    )
    gate_weight = jnp.sum(received.astype(jnp.float32), axis=2).reshape(buffer_rows, 1)
    d_act = gate_weight * near_rows
    d_gate = (d_act * pre_up * slope).astype(jnp.bfloat16)
    d_up = (d_act * silu_gate).astype(jnp.bfloat16)
    contract = (((1,), (1,)), ((), ()))
    pick_grad = lax.dot_general(d_gate, gate_matrix, contract, preferred_element_type=jnp.float32)
    pick_grad = (
        pick_grad + lax.dot_general(d_up, up_matrix, contract, preferred_element_type=jnp.float32)
    ).astype(jnp.bfloat16)
    gate_grad = jnp.sum(activation.astype(jnp.float32) * near_rows, axis=1).astype(jnp.bfloat16)
    back_rows, back_gate = (
        lax.all_to_all(
            pick_grad.reshape(expert_count, capacity, model_width),
            "exp",
            split_axis=0,
            concat_axis=0,
            tiled=True,
        ),
        lax.all_to_all(
            gate_grad.reshape(expert_count, capacity),
            "exp",
            split_axis=0,
            concat_axis=0,
            tiled=True,
        ),
    )
    picked_rows = back_rows.reshape(buffer_rows, model_width)[target]
    d_normed = jnp.sum(
        picked_rows.reshape(token_count, top_count, model_width).astype(jnp.float32), axis=1
    )
    picked_gate = (
        back_gate.reshape(buffer_rows)[target].astype(jnp.float32).reshape(token_count, top_count)
    )
    d_logit = gate_values * (
        picked_gate - jnp.sum(gate_values * picked_gate, axis=1, keepdims=True)
    )
    dense_logit = jnp.einsum("nk,nke->ne", d_logit, onehot, precision=highest)
    d_normed = d_normed + jnp.einsum(
        "ne,de->nd", dense_logit, router.astype(jnp.float32), precision=highest
    )
    grad_flat = norm_back(flat_rows, inverse, norm_gain, d_normed)
    grad_hidden = (
        grad_flat.reshape(1, local_passages, local_positions, model_width)
        + d_vector[None, :, None, :]
    )
    return (
        loss_value.reshape(1),
        own_score.reshape(1, local_passages),
        grad_hidden.astype(jnp.bfloat16),
    )


CORE, ACROSS_X, ACROSS_Y = 1, 2, 4
forward = (((1,), (0,)), ((), ()))
across = (((1,), (1,)), ((), ()))
MIB = 1 << 20


def swap(value, bit, size=8):
    return lax.ppermute(value, "exp", [(index, index ^ bit) for index in range(size)])


def shape_of(shape, dtype):
    return jax.ShapeDtypeStruct(shape, dtype)


def after(value, *others):
    return lax.optimization_barrier((value, *others))[0]


def kept(shape, dtype):
    return pltpu.VMEM(shape, dtype)


def pinned(array):
    return pltpu.with_memory_space_constraint(array, pltpu.VMEM)


def kernel_call(body, name, outs, ins, far=(), scratch=(), result=pltpu.VMEM):
    spaces = [pltpu.VMEM] * len(ins)
    ins = list(ins)
    for index in far:
        spaces[index] = pl.ANY
        ins[index] = pltpu.with_memory_space_constraint(ins[index], pltpu.HBM)
    return pl.pallas_call(
        body,
        name=name,
        out_shape=outs,
        in_specs=[pl.BlockSpec(memory_space=space) for space in spaces],
        out_specs=[pl.BlockSpec(memory_space=result)] * len(outs),
        scratch_shapes=scratch,
        compiler_params=pltpu.CompilerParams(vmem_limit_bytes=8 * MIB),
        cost_estimate=pl.CostEstimate(flops=1, bytes_accessed=1, transcendentals=0),
    )(*ins)


def split_low(values):
    high = values.astype(jnp.bfloat16)
    rest = values - high.astype(jnp.float32)
    middle = rest.astype(jnp.bfloat16)
    low = (rest - middle.astype(jnp.float32)).astype(jnp.bfloat16)
    return high, middle, low


def exact_dot(values, low_matrix, contract):
    parts = lax.dot_general(
        jnp.concatenate(split_low(values), axis=0),
        low_matrix,
        contract,
        preferred_element_type=jnp.float32,
    )
    return parts[0:8] + parts[8:16] + parts[16:24]


def other_order(values, bits):
    return jnp.concatenate([values[row ^ bits : (row ^ bits) + 1] for row in range(4)], axis=0)


def norm_kernel(
    hidden_far, gain_far, router_far, final_far, vector_far,
    hidden_ref, gain_ref, router_ref, normed_ref, sums_ref, head_ref,
    final_ref, vector_ref, copy_sems,
):
    pairs = (
        (hidden_far, hidden_ref), (gain_far, gain_ref), (router_far, router_ref),
        (final_far, final_ref), (vector_far, vector_ref),
    )
    copies = [
        pltpu.make_async_copy(source, target, copy_sems.at[index])
        for index, (source, target) in enumerate(pairs)
    ]
    for copy in copies:
        copy.start()
    for copy in copies:
        copy.wait()
    vector = vector_ref[...].astype(jnp.float32)
    vector = jnp.concatenate([vector[row : row + 1] for row in range(vector.shape[0])], axis=1)
    head_ref[...] = final_ref[...] * vector
    rows = hidden_ref[...].astype(jnp.float32)
    normed_ref[...] = (rows * rms_scale(rows) * gain_ref[...]).astype(jnp.bfloat16)
    sums_ref[...] = jnp.sum(rows, axis=0, keepdims=True)


def front_kernel(stage, owners, sets, count, router_ref, *refs):
    matrices, refs = refs[: 2 * len(sets)], refs[2 * len(sets) :]
    pieces, refs = refs[:count], refs[count:]
    matrices = list(matrices)
    hidden_units = matrices[0].shape[1]
    tile = 256
    firsts = range(0, hidden_units, tile)
    if stage == 0:
        far_matrices = matrices
        *refs, gate_held, up_held, rows_ref, copy_sems = refs
        matrices = [gate_held, up_held]
        copies = [
            pltpu.make_async_copy(
                source.at[:, first : first + tile],
                target.at[:, first : first + tile],
                copy_sems.at[which, number],
            )
            for number, first in enumerate(firsts)
            for which, (source, target) in enumerate(zip(far_matrices, matrices))
        ]
        for copy in copies:
            copy.start()
        turned_ref, *refs = refs
    elif stage == 3:
        sums_ref, *downs = refs[:3]
        earlier, refs = refs[3:6], refs[6:]
        *refs, terms_ref, rows_ref = refs
    else:
        *refs, rows_ref = refs
    gates_ref, *outs = refs
    expert = lax.axis_index("exp")
    first = 0
    for piece in pieces:
        rows_ref[first : first + piece.shape[0], :] = piece[...]
        first += piece.shape[0]
    size = first // len(owners)
    logits = lax.dot_general(
        rows_ref[...], router_ref[...], across, preferred_element_type=jnp.float32
    )
    weights = jnp.exp(logits)
    gates = weights / jnp.sum(weights, axis=1, keepdims=True)
    gates_ref[...] = gates
    lane = lax.broadcasted_iota(jnp.int32, gates.shape, 1)
    if stage == 0:
        weights = jnp.exp(
            lax.dot_general(
                router_ref[...], rows_ref[...], across, preferred_element_type=jnp.float32
            )
        )
        turned_ref[...] = weights / jnp.sum(weights, axis=0, keepdims=True)

    totals = []
    for place, which in enumerate(sets):
        gate_ref, up_ref = matrices[2 * place : 2 * place + 2]
        if stage == 3:
            slope_ref, silu_ref, act_ref = outs[3 * place : 3 * place + 3]
        else:
            slope_ref, silu_ref, act_ref, part_ref = outs
        own = jnp.sum(jnp.where(lane == expert ^ which, gates, 0.0), axis=1, keepdims=True)
        low = own.astype(jnp.bfloat16).astype(jnp.float32)
        parts = []
        for number, first in enumerate(firsts):
            columns = slice(first, first + tile)
            if stage == 0:
                copies[2 * number].wait()
                copies[2 * number + 1].wait()
            rows = rows_ref[...]
            pre_gate = jnp.dot(rows, gate_ref[:, columns], preferred_element_type=jnp.float32)
            pre_up = jnp.dot(rows, up_ref[:, columns], preferred_element_type=jnp.float32)
            silu_gate, slope = gate_parts(pre_gate)
            activation = (silu_gate * pre_up).astype(jnp.bfloat16)
            slope_ref[:, columns] = slope * pre_up
            silu_ref[:, columns] = silu_gate
            act_ref[:, columns] = activation
            weighted = activation.astype(jnp.float32) * low
            found = {
                owner: jnp.sum(weighted[index * size : (index + 1) * size], axis=0, keepdims=True)
                for index, owner in enumerate(owners)
            }
            nothing = jnp.zeros_like(weighted[:1])
            parts.append(
                jnp.concatenate([found.get(owner, nothing) for owner in range(8)], axis=0)
            )
        totals.append(jnp.concatenate(parts, axis=1))
    if stage < 3:
        part_ref[...] = totals[0]
        return
    own_first, own_second, other_first = earlier
    totals[0] = totals[0] + (own_first[...] + own_second[...])
    totals[1] = totals[1] + other_first[...]
    terms = exact_dot(totals[0], downs[0][...], forward) + exact_dot(
        totals[1], downs[1][...], forward
    )
    row = lax.broadcasted_iota(jnp.int32, terms.shape, 0)
    terms_ref[...] = (terms + jnp.where(row == 0, sums_ref[...], 0.0))[:4]


def front(stage, owners, sets, pieces, router_rows, matrices, more=()):
    model_width, hidden_units = matrices[0].shape
    row_total = sum(piece.shape[0] for piece in pieces)
    outs = [kept((row_total, 8), jnp.float32)]
    if stage == 0:
        outs.insert(0, kept((8, row_total), jnp.float32))
    for which in sets:
        outs += [
            kept((row_total, hidden_units), jnp.float32),
            kept((row_total, hidden_units), jnp.float32),
            kept((row_total, hidden_units), jnp.bfloat16),
        ]
    outs.append(
        kept((4, model_width), jnp.float32) if stage == 3 else kept((8, hidden_units), jnp.float32)
    )
    scratch = [pltpu.VMEM((row_total, model_width), jnp.bfloat16)]
    far = ()
    if stage == 0:
        far = (1, 2)
        outs += [kept(matrix.shape, jnp.bfloat16) for matrix in matrices]
        scratch.append(pltpu.SemaphoreType.DMA((2, hidden_units // 256)))
    else:
        matrices = [pinned(matrix) for matrix in matrices]
    if stage == 3:
        more = [pinned(array) for array in more]
    return kernel_call(
        functools.partial(front_kernel, stage, owners, sets, len(pieces)),
        "front",
        outs,
        [pinned(router_rows), *matrices, *(pinned(piece) for piece in pieces), *more],
        far,
        scratch,
    )


def near_kernel(
    own_ref, x_ref, y_ref, far_ref, head_ref, down_ref, other_down_ref,
    near_ref, other_near_ref, unit_ref, score_ref, own_score_ref, *, token_count,
):
    pooled = (
        (own_ref[...] + other_order(x_ref[...], 1))
        + (other_order(y_ref[...], 2) + other_order(far_ref[...], 3))
    ) / token_count
    pooled = jnp.concatenate([pooled, jnp.zeros_like(pooled)], axis=0)
    head = head_ref[...]
    scale = rms_scale(pooled)
    along = jnp.sum(pooled * head, axis=1, keepdims=True)
    own_score = (scale * along)[:1]
    own_score_ref[...] = own_score
    score_ref[...] = jnp.broadcast_to(own_score, score_ref.shape)
    unit = (
        scale * head - scale * scale * scale * (along / pooled.shape[1]) * pooled
    ) / token_count
    unit_ref[...] = unit[:1]
    near_ref[...] = exact_dot(unit, down_ref[...], forward)
    other_near_ref[...] = exact_dot(unit, other_down_ref[...], forward)


def back_kernel(passages, gate_count, saved_count, near_ref, other_near_ref, *refs):
    gates_refs, refs = refs[:gate_count], refs[gate_count:]
    saved, refs = refs[: 3 * saved_count], refs[3 * saved_count :]
    matrices, refs = refs[:4], refs[4:]
    *out_refs, d_gate_ref, d_up_ref, other_d_gate_ref, other_d_up_ref = refs
    expert = lax.axis_index("exp")
    size = out_refs[0].shape[1]
    model_width = matrices[0].shape[1]
    lane = lax.broadcasted_iota(jnp.int32, (size, 8), 1)
    line = lax.broadcasted_iota(jnp.int32, (16, size), 0)
    experts = (
        (near_ref, d_gate_ref, d_up_ref), (other_near_ref, other_d_gate_ref, other_d_up_ref)
    )
    sides = (d_gate_ref, d_up_ref, other_d_gate_ref, other_d_up_ref)
    for index, (owner, gates_place, saved_places, windows, unused) in enumerate(passages):
        rows = slice(index * size, (index + 1) * size)
        lines = jnp.zeros((16, size), jnp.float32)
        gates = gates_refs[gates_place[0]][gates_place[1] : gates_place[1] + size, :]
        for which, (table_ref, d_gate_out, d_up_out) in enumerate(experts):
            number, first = saved_places[which]
            slope_ref, silu_ref, act_ref = saved[3 * number : 3 * number + 3]
            held = slice(first, first + size)
            near = table_ref[owner : owner + 1, :]
            own = jnp.sum(
                jnp.where(lane == expert ^ which, gates, 0.0), axis=1, keepdims=True
            )
            d_act = own.astype(jnp.bfloat16).astype(jnp.float32) * near
            d_gate_out[rows, :] = (d_act * slope_ref[held, :]).astype(jnp.bfloat16)
            d_up_out[rows, :] = (d_act * silu_ref[held, :]).astype(jnp.bfloat16)
            if windows[-1][1] == model_width:
                gate_grad = exact_dot(table_ref[...], act_ref[held, :], across)
                lines = jnp.where(line == expert ^ which, gate_grad[owner : owner + 1], lines)
        for start, stop in windows:
            out_ref, *out_refs = out_refs
            used = stop - start
            if stop == model_width:
                out_ref[used : used + 16, :] = lines.astype(jnp.bfloat16)
                used += 16
            if out_ref.shape[0] > used:
                out_ref[used:, :] = jnp.zeros((out_ref.shape[0] - used, size), jnp.bfloat16)
            for first in range(start, stop, 256):
                pick_grad = None
                for side_ref, matrix in zip(sides, matrices):
                    term = jnp.dot(
                        side_ref[rows, :],
                        matrix[:, first : first + 256],
                        preferred_element_type=jnp.float32,
                    )
                    pick_grad = term if pick_grad is None else pick_grad + term
                out_ref[first - start : first - start + 256, :] = pick_grad.T.astype(jnp.bfloat16)


def back(passages, near, other_near, gates, saved, matrices, size):
    hidden_units, model_width = matrices[0].shape
    heights = [
        max(least, stop - start + (16 if stop == model_width else 0))
        for passage in passages
        for (start, stop), least in zip(*passage[3:])
    ]
    arrays = [array for group in saved for array in group]
    return kernel_call(
        functools.partial(back_kernel, passages, len(gates), len(saved)),
        "back",
        [kept((height, size), jnp.bfloat16) for height in heights],
        [pinned(array) for array in (near, other_near, *gates, *arrays, *matrices)],
        (),
        [pltpu.VMEM((len(passages) * size, hidden_units), jnp.bfloat16)] * 4,
    )


def add_kernel(x_ref, y_ref, high_ref, low_ref, x_out, y_out):
    for own_ref, other_ref, out_ref in ((x_ref, high_ref, x_out), (y_ref, low_ref, y_out)):
        out_ref[...] = (
            own_ref[...].astype(jnp.float32)
            + other_ref[: own_ref.shape[0], :].astype(jnp.float32)
        ).astype(jnp.bfloat16)


def turn_kernel(*refs):
    count = len(refs) // 2
    for source_ref, target_ref in zip(refs[:count], refs[count:]):
        for first in range(0, source_ref.shape[0], 256):
            rows = slice(first, first + 256)
            target_ref[:, rows] = source_ref[rows, :].T


def turn(matrices):
    return kernel_call(
        turn_kernel,
        "turn",
        [kept(matrix.shape[::-1], jnp.bfloat16) for matrix in matrices],
        [pinned(matrix) for matrix in matrices],
    )


def half_kernel(part, rows_ref, out_ref):
    half = out_ref.shape[0]
    out_ref[...] = rows_ref[part * half : (part + 1) * half, :]


def half_of(rows, part):
    total, wide = rows.shape
    (out,) = kernel_call(
        functools.partial(half_kernel, part), "half", [kept((total // 2, wide), rows.dtype)], [rows]
    )
    return out


def pack_kernel(first_ref, second_ref, out_ref):
    out_ref[:1, :] = first_ref[:1, :]
    out_ref[1:, :] = second_ref[:1, :]


def pack(first, second):
    return kernel_call(
        pack_kernel, "pack", [kept((2, first.shape[1]), first.dtype)], [pinned(first), second]
    )[0]


def pairs_of(passages):
    row = lax.broadcasted_iota(jnp.int32, (8, 128), 0)
    lane = lax.broadcasted_iota(jnp.int32, (8, 128), 1)
    return row, lane, jnp.logical_and(row < passages, lane < passages)


def spread(index, values):
    total = jnp.zeros((8, 128), jnp.float32)
    for number, value in values:
        total = jnp.where(index == number, value, total)
    return total


def whole_sum(values):
    return jnp.sum(jnp.sum(values, axis=1, keepdims=True), axis=0, keepdims=True)


def pair_kernel(
    grades_far, ranks_far, down_far, swap_gain_ref, down_ref, grades_ref, ranks_ref, copy_sems
):
    down_copy = pltpu.make_async_copy(down_far, down_ref, copy_sems.at[2])
    down_copy.start()
    copies = [
        pltpu.make_async_copy(grades_far, grades_ref, copy_sems.at[0]),
        pltpu.make_async_copy(ranks_far, ranks_ref, copy_sems.at[1]),
    ]
    for copy in copies:
        copy.start()
    for copy in copies:
        copy.wait()
    passages = grades_ref.shape[1]
    row, lane, pair = pairs_of(passages)
    grade_list = [(number, grades_ref[0, number].astype(jnp.float32)) for number in range(passages)]
    rank_list = [(number, ranks_ref[0, number].astype(jnp.float32)) for number in range(passages)]
    grade_row, grade_lane = spread(row, grade_list), spread(lane, grade_list)
    worth_row, worth_lane = jnp.exp2(grade_row), jnp.exp2(grade_lane)
    discount_row = 1.0 / jnp.log2(2.0 + spread(row, rank_list))
    discount_lane = 1.0 / jnp.log2(2.0 + spread(lane, rank_list))
    ahead = jnp.logical_or(
        grade_lane > grade_row, jnp.logical_and(grade_lane == grade_row, lane < row)
    )
    ideal_rank = jnp.sum(
        jnp.where(jnp.logical_and(pair, ahead), 1.0, 0.0), axis=1, keepdims=True
    )
    ideal_terms = (worth_row - 1.0) / jnp.log2(2.0 + ideal_rank)
    one_lane = jnp.logical_and(pair, lane == 0)
    ideal_gain = whole_sum(jnp.where(one_lane, ideal_terms, 0.0))
    swap_gain = (
        jnp.abs((worth_row - worth_lane) * (discount_row - discount_lane)) / ideal_gain
    )
    swap_gain_ref[...] = jnp.where(
        jnp.logical_and(pair, grade_row > grade_lane), swap_gain, 0.0
    )
    down_copy.wait()


def rank_kernel(swap_gain_ref, near_scores_ref, far_scores_ref, loss_ref, factor_ref):
    passages = 2 * near_scores_ref.shape[0]
    place = lax.axis_index("psg")
    row, lane, unused = pairs_of(passages)
    score_list = [
        (place ^ (base + number), jnp.broadcast_to(ref[number : number + 1, :], (8, 128)))
        for base, ref in ((0, near_scores_ref), (passages // 2, far_scores_ref))
        for number in range(passages // 2)
    ]
    swap_gain = swap_gain_ref[...]
    margin = spread(row, score_list) - spread(lane, score_list)
    softplus = jnp.maximum(-margin, 0.0) + jnp.log1p(jnp.exp(-jnp.abs(margin)))
    loss_ref[...] = whole_sum(swap_gain * softplus)
    pull = swap_gain * jax.nn.sigmoid(-margin)
    gradient = whole_sum(jnp.where(lane == place, pull, 0.0) - jnp.where(row == place, pull, 0.0))
    factor_ref[...] = jnp.broadcast_to(gradient * loss_scale, factor_ref.shape)


def first_end_kernel(own_ref, x_low_ref, y_high_ref, total_ref, lines_ref):
    model_width = total_ref.shape[1]
    cut = model_width // 2
    for first in range(0, model_width, 256):
        rows = slice(first, first + 256)
        if first < cut:
            term = x_low_ref[rows, :]
        else:
            term = y_high_ref[first - cut : first - cut + 256, :]
        total = own_ref[rows, :].astype(jnp.float32) + term.astype(jnp.float32)
        total_ref[:, rows] = total.T
    end = slice(model_width, model_width + 8)
    end_high = slice(model_width - cut, model_width - cut + 8)
    lines_ref[...] = own_ref[end, :].astype(jnp.float32) + y_high_ref[end_high, :].astype(
        jnp.float32
    )


def end_kernel(
    factor_ref, total_ref, lines_ref, x_high_ref, y_low_ref,
    hidden_ref, gain_ref, gates_ref, router_ref, unit_ref,
    grad_far, turned_ref, grad_ref, copy_sems,
):
    token_count, model_width = hidden_ref.shape
    cut = y_low_ref.shape[0]
    end_high = slice(model_width - cut, model_width - cut + 8)
    slot_grad = lines_ref[...] + x_high_ref[end_high, :].astype(jnp.float32)
    gates = gates_ref[...]
    d_logit = gates * (slot_grad - jnp.sum(gates * slot_grad, axis=0, keepdims=True))
    d_logit = jnp.concatenate([d_logit, jnp.zeros((120, token_count), jnp.float32)], axis=0).T
    d_logit = jnp.concatenate(split_low(d_logit[:, :8]), axis=1)
    router_rows = jnp.concatenate([router_ref[...]] * 3, axis=0)
    for first in range(0, model_width, 256):
        columns = slice(first, first + 256)
        if first < cut:
            term = y_low_ref[columns, :]
        else:
            term = x_high_ref[first - cut : first - cut + 256, :]
        turned_ref[:, columns] = (
            total_ref[:, columns]
            + term.astype(jnp.float32).T
            + jnp.dot(d_logit, router_rows[:, columns], preferred_element_type=jnp.float32)
        )
    gain = gain_ref[...]
    factor = factor_ref[:, :1]
    size = 16
    copies = []
    for first in range(0, token_count, size):
        rows = slice(first, first + size)
        flat_rows = hidden_ref[rows, :].astype(jnp.float32)
        grad = norm_back(flat_rows, rms_scale(flat_rows), gain, turned_ref[rows, :])
        grad_ref[rows, :] = ((grad + unit_ref[...]) * factor).astype(jnp.bfloat16)
        copies.append(
            pltpu.make_async_copy(
                grad_ref.at[rows, :], grad_far.at[rows, :], copy_sems.at[first // size]
            )
        )
        copies[-1].start()
    for copy in copies:
        copy.wait()


def every_expert(
    hidden,
    norm_gain,
    router,
    gate_proj,
    up_proj,
    down_proj,
    final_gain,
    score_vector,
    expert_ids,
    grades,
    passage_ranks,
):
    unused_query, unused_passage, token_count, model_width = hidden.shape
    passages = grades.shape[1]
    flat = hidden.reshape(token_count, model_width)
    gate_matrix, up_matrix, down_matrix = gate_proj[0], up_proj[0], down_proj[0]
    mine = [gate_matrix, up_matrix, down_matrix]
    flat, gain, router_rows, normed, token_sums, head = kernel_call(
        norm_kernel,
        "norm",
        [
            kept(flat.shape, jnp.bfloat16),
            kept((1, model_width), jnp.float32),
            kept((8, model_width), jnp.bfloat16),
            kept(flat.shape, jnp.bfloat16),
            kept((1, model_width), jnp.float32),
            kept((1, model_width), jnp.float32),
        ],
        [
            flat,
            norm_gain.reshape(1, model_width),
            router.T,
            final_gain.reshape(1, model_width),
            score_vector.reshape(model_width // 128, 128),
        ],
        range(5),
        [
            pltpu.VMEM((1, model_width), jnp.float32),
            pltpu.VMEM((model_width // 128, 128), jnp.bfloat16),
            pltpu.SemaphoreType.DMA((5,)),
        ],
    )
    others = [swap(matrix, CORE) for matrix in mine]
    x_rows, y_rows = swap(normed, ACROSS_X), swap(normed, ACROSS_Y)
    turned_gates, own_gates, *own_saved, own_part, mine[0], mine[1] = front(
        0, (0,), (0,), [normed], router_rows, mine[:2]
    )
    swap_gain, mine[2] = kernel_call(
        pair_kernel,
        "pairs",
        [kept((8, 128), jnp.float32), kept(down_matrix.shape, jnp.bfloat16)],
        [grades, after(passage_ranks, own_part), down_matrix],
        (0, 1, 2),
        [
            pltpu.SMEM(grades.shape, jnp.int32),
            pltpu.SMEM(grades.shape, jnp.int32),
            pltpu.SemaphoreType.DMA((3,)),
        ],
    )
    *mine_turned, down_turned = turn(mine)
    x_rows, y_rows = after(x_rows, mine_turned[0]), after(y_rows, mine_turned[0])
    far_low = swap(half_of(x_rows, 0), ACROSS_Y)
    far_high = swap(half_of(y_rows, 1), ACROSS_X)
    side_gates, *side_saved, side_part = front(
        1, (1, 2), (0,), [x_rows, y_rows], router_rows, mine[:2]
    )
    others[0] = after(others[0], side_part)
    unused, *other_saved, other_part = front(
        2, (0, 1, 2), (1,), [normed, x_rows, y_rows], router_rows, others[:2]
    )
    far_low, far_high = after(far_low, other_part), after(far_high, other_part)
    far_gates, *far_saved, terms = front(
        3, (3,), (0, 1), [far_low, far_high], router_rows, mine[:2] + others[:2],
        (token_sums, mine[2], others[2], own_part, side_part, other_part),
    )

    *others_turned, other_down_turned = turn([after(others[0], terms), *others[1:]])
    head = after(head, others_turned[0])
    near, other_near, unit_vector, travelling, own_score = kernel_call(
        functools.partial(near_kernel, token_count=token_count),
        "near",
        [
            kept((8, down_matrix.shape[0]), jnp.float32),
            kept((8, down_matrix.shape[0]), jnp.float32),
            kept((1, model_width), jnp.float32),
            kept((1, 128), jnp.float32),
            shape_of((1, 1), jnp.float32),
        ],
        [
            pinned(terms),
            swap(terms, ACROSS_X),
            swap(terms, ACROSS_Y),
            swap(terms, ACROSS_X | ACROSS_Y),
            pinned(head),
            pinned(down_turned),
            pinned(other_down_turned),
        ],
    )
    matrices = [*mine_turned, *others_turned]
    middle = model_width // 2
    lower, upper, early, earlier = (0, middle), (middle, model_width), middle + 32, middle + 64
    far_low, far_high = back(
        ((3, (0, 0), ((0, 0), (1, 0)), (lower, upper), (earlier, earlier)),),
        near, other_near, [far_gates], [far_saved[:3], far_saved[3:]], matrices, token_count,
    )
    far_sent = far_low
    far_low, far_high = swap(far_low, ACROSS_X), swap(far_high, ACROSS_Y)

    def sides_back(x_window, y_window, least, *earlier):
        return back(
            (
                (1, (0, 0), ((0, 0), (1, token_count)), (x_window,), (least,)),
                (2, (0, token_count), ((0, token_count), (1, 2 * token_count)), (y_window,), (least,)),
            ),
            after(near, *earlier), other_near, [side_gates], [side_saved, other_saved], matrices,
            token_count,
        )

    x_low, y_high = sides_back(lower, upper, early, far_sent)
    first_sent = x_low
    x_low, y_high = swap(x_low, ACROSS_X), swap(y_high, ACROSS_Y)
    x_high, y_low = sides_back(upper, lower, 0, first_sent)
    travelling = after(travelling, first_sent)
    met = lax.ppermute(travelling, "psg", [(index, index ^ 1) for index in range(passages)])
    near_scores = pack(travelling, met)
    far_high = after(far_high, near_scores)
    x_high, y_low = kernel_call(
        add_kernel,
        "add",
        [kept(x_high.shape, jnp.bfloat16), kept(y_low.shape, jnp.bfloat16)],
        [pinned(x_high), pinned(y_low), far_high, far_low],
    )
    x_high, y_low, near_scores, other_near = lax.optimization_barrier(
        (x_high, y_low, near_scores, other_near)
    )
    x_high, y_low = swap(x_high, ACROSS_X), swap(y_low, ACROSS_Y)
    (own_sums,) = back(
        ((0, (0, 0), ((0, 0), (1, 0)), ((0, model_width),), (0,)),),
        near, other_near, [own_gates], [own_saved, other_saved], matrices, token_count,
    )
    far_scores = lax.ppermute(near_scores, "psg", [(index, index ^ 2) for index in range(passages)])
    loss, factor = kernel_call(
        rank_kernel,
        "rank",
        [shape_of((1, 1), jnp.float32), kept((1, 128), jnp.float32)],
        [pinned(swap_gain), pinned(near_scores), far_scores],
    )
    total, lines = kernel_call(
        first_end_kernel,
        "first_end",
        [
            kept((token_count, model_width), jnp.float32),
            kept((8, token_count), jnp.float32),
        ],
        [pinned(own_sums), after(x_low, factor), y_high],
    )
    (grad,) = kernel_call(
        end_kernel,
        "end",
        [shape_of((token_count, model_width), jnp.bfloat16)],
        [
            pinned(factor), pinned(total), pinned(lines), x_high, y_low, pinned(flat), pinned(gain),
            pinned(turned_gates), pinned(router_rows), pinned(unit_vector),
        ],
        scratch=[
            pltpu.VMEM((token_count, model_width), jnp.float32),
            pltpu.VMEM((token_count, model_width), jnp.bfloat16),
            pltpu.SemaphoreType.DMA((token_count // 16,)),
        ],
        result=pl.ANY,
    )
    return (loss.reshape(1), own_score, grad.reshape(hidden.shape))


def block(*arrays):
    hidden, router, expert_ids, grades = arrays[0], arrays[2], arrays[8], arrays[9]
    each_expert = router.shape[1] == expert_ids.shape[3] == 8
    if hidden.shape[1] == 1 and each_expert and grades.shape[1] == 4:
        return every_expert(*arrays)
    return local(*arrays)


def solution(mesh):
    placed = (
        P("exp", "psg", None, None),
        P(),
        P(),
        P("exp", None, None),
        P("exp", None, None),
        P("exp", None, None),
        P(),
        P(),
        P("exp", "psg", None, None),
        P("exp", None),
        P("exp", None),
    )
    return jax.shard_map(
        block,
        mesh=mesh,
        in_specs=placed,
        out_specs=(P("exp"), P("exp", "psg"), P("exp", "psg", None, None)),
        check_vma=False,
    )
```

profile of v0, /device:TPU:0, one launch (start us, length us, event | category | flops | bytes accessed | tf_op | source)
XLA Modules:
  0.0 61.7 jit_solution(1713874345384274726)
XLA Ops:
  1.7 1.4 %norm.1 = (bf16[128,2048]{1,0:T(8,128)(2,1)S(1)}, f32[1,2048]{1,0:T(1,128)S(1)}, bf16[8,2048]{1,0:T(8,128)(2,1)S(1)}, bf16[128,2048]{1,0:T(8,128)(2,1)S(1)}, f32...) custom-call(bf16[128,2048]{1,0:T(8,128)(2,1)} %bitcast.16, f32[1,2048]{1,0:T(1,128)} %bitcast.19, bf16[8,2048]{1,0:T(8,128)(2,1)} %bitcast.18, ...), custom_call_target="tpu_custom_call" | custom-call | flops 1 | bytes 1 | tf_op jit(solution)/shard_map/norm/pallas_call | solution.py:244
  3.1 2.7 %collective-permute-start.2 = (bf16[128,2048]{1,0:T(8,128)(2,1)S(1)}, bf16[128,2048]{1,0:T(8,128)(2,1)S(1)}, u32[]{:S(2)}, u32[]{:S(2)}) collective-permute-start(bf16[128,2048]{1,0:T(8,128)(2,1)S(1)} %get-tuple-element.77.refs_2_), channel_id=1, source_target_pairs={{0,4},{1,5},{2,6},{3,7},{4,0},{5,1},{6,2},{7,3},{8,12},{9,13},{10,... | collective-permute-start | bytes 1572872 | tf_op jit(solution)/shard_map/ppermute | solution.py:219
  5.7 1.5 %collective-permute-start.1 = (bf16[128,2048]{1,0:T(8,128)(2,1)S(1)}, bf16[128,2048]{1,0:T(8,128)(2,1)S(1)}, u32[]{:S(2)}, u32[]{:S(2)}) collective-permute-start(bf16[128,2048]{1,0:T(8,128)(2,1)S(1)} %get-tuple-element.77.refs_2_), channel_id=1, source_target_pairs={{0,2},{1,3},{2,0},{3,1},{4,6},{5,7},{6,4},{7,5},{8,10},{9,11},{10,... | collective-permute-start | bytes 1572872 | tf_op jit(solution)/shard_map/ppermute | solution.py:219
  7.2 3.7 %front.4 = (f32[8,128]{1,0:T(8,128)S(1)}, f32[128,8]{1,0:T(8,128)S(1)}, f32[128,768]{1,0:T(8,128)S(1)}, f32[128,768]{1,0:T(8,128)S(1)}, bf16[128,768]{1,0:T(8,12...) custom-call(bf16[8,2048]{1,0:T(8,128)(2,1)S(1)} %get-tuple-element.76.router_ref, ...), custom_call_target="tpu_custom_call" | custom-call | flops 1 | bytes 1 | tf_op jit(solution)/shard_map/front/pallas_call | solution.py:244
  11.0 1.9 %pairs.1 = (f32[8,128]{1,0:T(8,128)S(1)}, bf16[768,2048]{1,0:T(8,128)(2,1)S(1)}) custom-call(s32[1,4]{1,0:T(1,128)} %grades_far.1, s32[1,4]{1,0:T(1,128)} %ranks_far, bf16[768,2048]{1,0:T(8,128)(2,1)} %bitcast.11), custom_call_target="tpu_custom_call" | custom-call | flops 1 | bytes 1 | tf_op jit(solution)/shard_map/pairs/pallas_call | solution.py:244
  12.9 2.6 %turn.2 = (bf16[768,2048]{1,0:T(8,128)(2,1)S(1)}, bf16[768,2048]{1,0:T(8,128)(2,1)S(1)}, bf16[2048,768]{1,0:T(8,128)(2,1)S(1)}) custom-call(bf16[2048,768]{1,0:T(8,128)(2,1)S(1)} %get-tuple-element.81.refs_0_, bf16[2048,768]{1,0:T(8,128)(2,1)S(1)} %get-tuple-element.82.refs_1_, bf16[768,2048]{1,0:T(8,128)(2,1)S(1)} %get-tuple-element.83.refs_2_.refs_7_), custom_call_target="tpu_custom_call" | custom-call | flops 1 | bytes 1 | tf_op jit(solution)/shard_map/turn/pallas_call | solution.py:244
  15.5 2.7 %collective-permute-done.2.refs_3_.refs_4_.rows_ref = bf16[128,2048]{1,0:T(8,128)(2,1)S(1)} collective-permute-done((bf16[128,2048]{1,0:T(8,128)(2,1)S(1)}, bf16[128,2048]{1,0:T(8,128)(2,1)S(1)}, u32[]{:S(2)}, u32[]{:S(2)}) %collective-permute-start.2) | collective-permute-done | bytes 524320 | tf_op jit(solution)/shard_map/ppermute | solution.py:219
  18.3 1.8 %collective-permute-start.5 = (bf16[64,2048]{1,0:T(8,128)(2,1)S(1)}, bf16[64,2048]{1,0:T(8,128)(2,1)S(1)}, u32[]{:S(2)}, u32[]{:S(2)}) collective-permute-start(bf16[64,2048]{1,0:T(8,128)(2,1)S(1)} %half.3), channel_id=1, source_target_pairs={{0,2},{1,3},{2,0},{3,1},{4,6},{5,7},{6,4},{7,5},{8,10},{9,11},{10,... | collective-permute-start | bytes 786440 | tf_op jit(solution)/shard_map/ppermute | solution.py:219
  20.1 1.6 %collective-permute-start.4 = (bf16[64,2048]{1,0:T(8,128)(2,1)S(1)}, bf16[64,2048]{1,0:T(8,128)(2,1)S(1)}, u32[]{:S(2)}, u32[]{:S(2)}) collective-permute-start(bf16[64,2048]{1,0:T(8,128)(2,1)S(1)} %half.2), channel_id=1, source_target_pairs={{0,4},{1,5},{2,6},{3,7},{4,0},{5,1},{6,2},{7,3},{8,12},{9,13},{10,... | collective-permute-start | bytes 786440 | tf_op jit(solution)/shard_map/ppermute | solution.py:219
  21.7 2.1 %front.5 = (f32[256,8]{1,0:T(8,128)S(1)}, f32[256,768]{1,0:T(8,128)S(1)}, f32[256,768]{1,0:T(8,128)S(1)}, bf16[256,768]{1,0:T(8,128)(2,1)S(1)}, f32[8,768]{1,0:T(8,128)S(1)}) custom-call(bf16[8,2048]{1,0:T(8,128)(2,1)S(1)} %get-tuple-element.76.router_ref, bf16[2048,768]{1,0:T(8,128)(2,1)S(1)} %get-tuple-element.81.refs_0_, ...), custom_call_target="tpu_custom_call" | custom-call | flops 1 | bytes 1 | tf_op jit(solution)/shard_map/front/pallas_call | solution.py:244
  23.8 3.4 %front.6 = (f32[384,8]{1,0:T(8,128)}, f32[384,768]{1,0:T(8,128)S(1)}, f32[384,768]{1,0:T(8,128)S(1)}, bf16[384,768]{1,0:T(8,128)(2,1)S(1)}, f32[8,768]{1,0:T(8,128)S(1)}) custom-call(bf16[8,2048]{1,0:T(8,128)(2,1)S(1)} %get-tuple-element.76.router_ref, bf16[2048,768]{1,0:T(8,128)(2,1)S(1)} %collective-permute-done.refs_0_.refs_2_, ...), custom_call_target="tpu_custom_call" | custom-call | flops 1 | bytes 1 | tf_op jit(solution)/shard_map/front/pallas_call | solution.py:244
  27.2 0.5 collective-permute-done.4.refs_4_
  27.7 3.0 %front.7 = (f32[128,8]{1,0:T(8,128)S(1)}, f32[128,768]{1,0:T(8,128)S(1)}, f32[128,768]{1,0:T(8,128)S(1)}, bf16[128,768]{1,0:T(8,128)(2,1)S(1)}, f32[128,768]{1,0...) custom-call(bf16[8,2048]{1,0:T(8,128)(2,1)S(1)} %get-tuple-element.76.router_ref, ...), custom_call_target="tpu_custom_call" | custom-call | flops 1 | bytes 1 | tf_op jit(solution)/shard_map/front/pallas_call | solution.py:244
  30.7 1.6 %collective-permute-start.9 = (f32[4,2048]{1,0:T(4,128)S(1)}, f32[4,2048]{1,0:T(4,128)S(1)}, u32[]{:S(2)}, u32[]{:S(2)}) collective-permute-start(f32[4,2048]{1,0:T(4,128)S(1)} %get-tuple-element.93.own_ref), channel_id=1, source_target_pairs={{0,6},{1,7},{2,4},{3,5},{4,2},{5,3},{6,0},{7,1},{8,14},{9,15},{10,... | collective-permute-start | bytes 98312 | tf_op jit(solution)/shard_map/ppermute | solution.py:219
  32.3 1.1 %collective-permute-start.8 = (f32[4,2048]{1,0:T(4,128)S(1)}, f32[4,2048]{1,0:T(4,128)S(1)}, u32[]{:S(2)}, u32[]{:S(2)}) collective-permute-start(f32[4,2048]{1,0:T(4,128)S(1)} %get-tuple-element.93.own_ref), channel_id=1, source_target_pairs={{0,4},{1,5},{2,6},{3,7},{4,0},{5,1},{6,2},{7,3},{8,12},{9,13},{10,... | collective-permute-start | bytes 98312 | tf_op jit(solution)/shard_map/ppermute | solution.py:219
  33.4 0.9 %collective-permute-start.7 = (f32[4,2048]{1,0:T(4,128)S(1)}, f32[4,2048]{1,0:T(4,128)S(1)}, u32[]{:S(2)}, u32[]{:S(2)}) collective-permute-start(f32[4,2048]{1,0:T(4,128)S(1)} %get-tuple-element.93.own_ref), channel_id=1, source_target_pairs={{0,2},{1,3},{2,0},{3,1},{4,6},{5,7},{6,4},{7,5},{8,10},{9,11},{10,... | collective-permute-start | bytes 98312 | tf_op jit(solution)/shard_map/ppermute | solution.py:219
  34.3 2.8 %turn.3 = (bf16[768,2048]{1,0:T(8,128)(2,1)S(1)}, bf16[768,2048]{1,0:T(8,128)(2,1)S(1)}, bf16[2048,768]{1,0:T(8,128)(2,1)S(1)}) custom-call(bf16[2048,768]{1,0:T(8,128)(2,1)S(1)} %collective-permute-done.refs_0_.refs_2_, bf16[2048,768]{1,0:T(8,128)(2,1)S(1)} %collective-permute-done.3.refs_1_.refs_3_, ...), custom_call_target="tpu_custom_call" | custom-call | flops 1 | bytes 1 | tf_op jit(solution)/shard_map/turn/pallas_call | solution.py:244
  37.3 1.7 %near.1 = (f32[8,768]{1,0:T(8,128)S(1)}, f32[8,768]{1,0:T(8,128)S(1)}, f32[1,2048]{1,0:T(1,128)S(1)}, f32[1,128]{1,0:T(1,128)S(1)}, f32[1,1]{1,0:T(1,128)}) custom-call(f32[4,2048]{1,0:T(4,128)S(1)} %get-tuple-element.93.own_ref, f32[4,2048]{1,0:T(4,128)S(1)} %collective-permute-done.7.x_ref, f32[4,2048]{1,0:T(4,128)S(1)} %collective-permute-done.8.y_ref, ...), custom_call_target="tpu_custom_call" | custom-call | flops 1 | bytes 1 | tf_op jit(solution)/shard_map/near/pallas_call | solution.py:244
  39.0 2.1 %back.4 = (bf16[1088,128]{1,0:T(8,128)(2,1)S(1)}, bf16[1088,128]{1,0:T(8,128)(2,1)S(1)}) custom-call(f32[8,768]{1,0:T(8,128)S(1)} %get-tuple-element.121.near_ref, f32[8,768]{1,0:T(8,128)S(1)} %get-tuple-element.134.other_near_ref, f32[128,8]{1,0:T(8,128)S(1)} %get-tuple-element.102.refs_0_, f32[128,768]{1,0:T(8,128)S(1)} %get-tuple-element.103.refs_1_, ...), custom_call_target="tpu_custom_call" | custom-call | flops 1 | bytes 1 | tf_op jit(solution)/shard_map/back/pallas_call | solution.py:244
  41.0 1.4 %collective-permute-start.10 = (bf16[1088,128]{1,0:T(8,128)(2,1)S(1)}, bf16[1088,128]{1,0:T(8,128)(2,1)S(1)}, u32[]{:S(2)}, u32[]{:S(2)}) collective-permute-start(bf16[1088,128]{1,0:T(8,128)(2,1)S(1)} %get-tuple-element.124), channel_id=1, source_target_pairs={{0,4},{1,5},{2,6},{3,7},{4,0},{5,1},{6,2},{7,3},{8,12},{9,13},{10,... | collective-permute-start | bytes 835592 | tf_op jit(solution)/shard_map/ppermute | solution.py:219
  42.5 1.1 %collective-permute-start.12 = (bf16[1088,128]{1,0:T(8,128)(2,1)S(1)}, bf16[1088,128]{1,0:T(8,128)(2,1)S(1)}, u32[]{:S(2)}, u32[]{:S(2)}) collective-permute-start(bf16[1088,128]{1,0:T(8,128)(2,1)S(1)} %get-tuple-element.111), channel_id=1, source_target_pairs={{0,2},{1,3},{2,0},{3,1},{4,6},{5,7},{6,4},{7,5},{8,10},{9,11},{10,... | collective-permute-start | bytes 835592 | tf_op jit(solution)/shard_map/ppermute | solution.py:219
  43.5 2.1 %back.5 = (bf16[1056,128]{1,0:T(8,128)(2,1)S(1)}, bf16[1056,128]{1,0:T(8,128)(2,1)S(1)}) custom-call(f32[8,768]{1,0:T(8,128)S(1)} %get-tuple-element.121.near_ref, f32[8,768]{1,0:T(8,128)S(1)} %get-tuple-element.134.other_near_ref, f32[256,8]{1,0:T(8,128)S(1)} %get-tuple-element.113.refs_0_, f32[256,768]{1,0:T(8,128)S(1)} %get-tuple-element.114.refs_1_, ...), custom_call_target="tpu_custom_call" | custom-call | flops 1 | bytes 1 | tf_op jit(solution)/shard_map/back/pallas_call | solution.py:244
  45.7 1.0 %collective-permute-start.14 = (bf16[1056,128]{1,0:T(8,128)(2,1)S(1)}, bf16[1056,128]{1,0:T(8,128)(2,1)S(1)}, u32[]{:S(2)}, u32[]{:S(2)}) collective-permute-start(bf16[1056,128]{1,0:T(8,128)(2,1)S(1)} %get-tuple-element.120), channel_id=1, source_target_pairs={{0,2},{1,3},{2,0},{3,1},{4,6},{5,7},{6,4},{7,5},{8,10},{9,11},{10,... | collective-permute-start | bytes 811016 | tf_op jit(solution)/shard_map/ppermute | solution.py:219
  46.7 0.7 %collective-permute-start.15 = (bf16[1056,128]{1,0:T(8,128)(2,1)S(1)}, bf16[1056,128]{1,0:T(8,128)(2,1)S(1)}, u32[]{:S(2)}, u32[]{:S(2)}) collective-permute-start(bf16[1056,128]{1,0:T(8,128)(2,1)S(1)} %get-tuple-element.140), channel_id=1, source_target_pairs={{0,4},{1,5},{2,6},{3,7},{4,0},{5,1},{6,2},{7,3},{8,12},{9,13},{10,... | collective-permute-start | bytes 811016 | tf_op jit(solution)/shard_map/ppermute | solution.py:219
  47.3 1.6 %collective-permute-start.11 = (f32[1,128]{1,0:T(1,128)S(1)}, f32[1,128]{1,0:T(1,128)S(1)}, u32[]{:S(2)}, u32[]{:S(2)}) collective-permute-start(f32[1,128]{1,0:T(1,128)S(1)} %get-tuple-element.126.first_ref), channel_id=1, source_target_pairs={{0,8},{8,0},{16,24},{24,16},{1,9},{9,1},{17,25},{25,17},{2,10},{10... | collective-permute-start | bytes 1544 | tf_op jit(solution)/shard_map/ppermute | solution.py:837
  48.9 2.1 %back.6 = (bf16[1040,128]{1,0:T(8,128)(2,1)S(1)}, bf16[1024,128]{1,0:T(8,128)(2,1)S(1)}) custom-call(f32[8,768]{1,0:T(8,128)S(1)} %get-tuple-element.121.near_ref, f32[8,768]{1,0:T(8,128)S(1)} %get-tuple-element.134.other_near_ref, f32[256,8]{1,0:T(8,128)S(1)} %get-tuple-element.113.refs_0_, f32[256,768]{1,0:T(8,128)S(1)} %get-tuple-element.114.refs_1_, ...), custom_call_target="tpu_custom_call" | custom-call | flops 1 | bytes 1 | tf_op jit(solution)/shard_map/back/pallas_call | solution.py:244
  51.0 1.0 %collective-permute-done.12.low_ref = bf16[1088,128]{1,0:T(8,128)(2,1)S(1)} collective-permute-done((bf16[1088,128]{1,0:T(8,128)(2,1)S(1)}, bf16[1088,128]{1,0:T(8,128)(2,1)S(1)}, u32[]{:S(2)}, u32[]{:S(2)}) %collective-permute-start.12) | collective-permute-done | bytes 278560 | tf_op jit(solution)/shard_map/ppermute | solution.py:219
  52.2 1.0 %collective-permute-start.16 = (bf16[1040,128]{1,0:T(8,128)(2,1)S(1)}, bf16[1040,128]{1,0:T(8,128)(2,1)S(1)}, u32[]{:S(2)}, u32[]{:S(2)}) collective-permute-start(bf16[1040,128]{1,0:T(8,128)(2,1)S(1)} %get-tuple-element.143), channel_id=1, source_target_pairs={{0,2},{1,3},{2,0},{3,1},{4,6},{5,7},{6,4},{7,5},{8,10},{9,11},{10,... | collective-permute-start | bytes 798728 | tf_op jit(solution)/shard_map/ppermute | solution.py:219
  53.7 2.6 %collective-permute-start.13 = (f32[2,128]{1,0:T(2,128)S(1)}, f32[2,128]{1,0:T(2,128)S(1)}, u32[]{:S(2)}, u32[]{:S(2)}) collective-permute-start(f32[2,128]{1,0:T(2,128)S(1)} %pack.1.near_scores_ref), channel_id=1, source_target_pairs={{0,16},{8,24},{16,0},{24,8},{1,17},{9,25},{17,1},{25,9},{2,18},{10... | collective-permute-start | bytes 3080 | tf_op jit(solution)/shard_map/ppermute | solution.py:854
  56.3 2.1 %back.7.own_ref = bf16[2064,128]{1,0:T(8,128)(2,1)S(1)} custom-call(f32[8,768]{1,0:T(8,128)S(1)} %get-tuple-element.121.near_ref, f32[8,768]{1,0:T(8,128)S(1)} %get-tuple-element.134.other_near_ref, f32[128,8]{1,0:T(8,128)S(1)} %get-tuple-element.135.refs_0_, f32[128,768]{1,0:T(8,128)S(1)} %get-tuple-element.136.refs_1_, ...), custom_call_target="tpu_custom_call" | custom-call | flops 1 | bytes 1 | tf_op jit(solution)/shard_map/back/pallas_call | solution.py:244
  58.4 0.6 %rank.1 = (f32[1,1]{1,0:T(1,128)}, f32[1,128]{1,0:T(1,128)S(1)}) custom-call(f32[8,128]{1,0:T(8,128)S(1)} %get-tuple-element.80.swap_gain_ref, f32[2,128]{1,0:T(2,128)S(1)} %pack.1.near_scores_ref, f32[2,128]{1,0:T(2,128)S(1)} %collective-permute-done.13.far_scores_ref), custom_call_target="tpu_custom_call" | custom-call | flops 1 | bytes 1 | tf_op jit(solution)/shard_map/rank/pallas_call | solution.py:244
  59.9 1.7 %end.1 = bf16[128,2048]{1,0:T(8,128)(2,1)} custom-call(f32[1,128]{1,0:T(1,128)S(1)} %get-tuple-element.133.factor_ref, f32[128,2048]{1,0:T(8,128)S(1)} %get-tuple-element.141.total_ref, f32[8,128]{1,0:T(8,128)S(1)} %get-tuple-element.142.lines_ref, bf16[1040,128]{1,0:T(8,128)(2,1)S(1)} %collective-permute-done.16.x_high_ref, ...), custom_call_target="tpu_custom_call" | custom-call | flops 1 | bytes 1 | tf_op jit(solution)/shard_map/end/pallas_call | solution.py:244
  (24 shorter events, 2.7 us)
Async XLA Ops:
  0.6 23.2 %collective-permute-start = (bf16[2048,768]{1,0:T(8,128)(2,1)}, bf16[2048,768]{1,0:T(8,128)(2,1)S(1)}, u32[]{:S(2)}, u32[]{:S(2)}) collective-permute-start(bf16[2048,768]{1,0:T(8,128)(2,1)} %bitcast.12), channel_id=1, source_target_pairs={{0,1},{1,0},{2,3},{3,2},{4,5},{5,4},{6,7},{7,6},{8,9},{9,8},{10,11... | collective-permute-start | bytes 9437192 | tf_op jit(solution)/shard_map/ppermute | solution.py:219
  1.1 22.7 %collective-permute-start.3 = (bf16[2048,768]{1,0:T(8,128)(2,1)}, bf16[2048,768]{1,0:T(8,128)(2,1)S(1)}, u32[]{:S(2)}, u32[]{:S(2)}) collective-permute-start(bf16[2048,768]{1,0:T(8,128)(2,1)} %bitcast.14), channel_id=1, source_target_pairs={{0,1},{1,0},{2,3},{3,2},{4,5},{5,4},{6,7},{7,6},{8,9},{9,8},{10,11... | collective-permute-start | bytes 9437192 | tf_op jit(solution)/shard_map/ppermute | solution.py:219
  1.2 26.5 %collective-permute-start.6 = (bf16[768,2048]{1,0:T(8,128)(2,1)}, bf16[768,2048]{1,0:T(8,128)(2,1)S(1)}, u32[]{:S(2)}, u32[]{:S(2)}) collective-permute-start(bf16[768,2048]{1,0:T(8,128)(2,1)} %bitcast.10), channel_id=1, source_target_pairs={{0,1},{1,0},{2,3},{3,2},{4,5},{5,4},{6,7},{7,6},{8,9},{9,8},{10,11... | collective-permute-start | bytes 9437192 | tf_op jit(solution)/shard_map/ppermute | solution.py:219
  3.1 15.2 %collective-permute-start.2 = (bf16[128,2048]{1,0:T(8,128)(2,1)S(1)}, bf16[128,2048]{1,0:T(8,128)(2,1)S(1)}, u32[]{:S(2)}, u32[]{:S(2)}) collective-permute-start(bf16[128,2048]{1,0:T(8,128)(2,1)S(1)} %get-tuple-element.77.refs_2_), channel_id=1, source_target_pairs={{0,4},{1,5},{2,6},{3,7},{4,0},{5,1},{6,2},{7,3},{8,12},{9,13},{10,... | collective-permute-start | bytes 1572872 | tf_op jit(solution)/shard_map/ppermute | solution.py:219
  5.7 14.3 %collective-permute-start.1 = (bf16[128,2048]{1,0:T(8,128)(2,1)S(1)}, bf16[128,2048]{1,0:T(8,128)(2,1)S(1)}, u32[]{:S(2)}, u32[]{:S(2)}) collective-permute-start(bf16[128,2048]{1,0:T(8,128)(2,1)S(1)} %get-tuple-element.77.refs_2_), channel_id=1, source_target_pairs={{0,2},{1,3},{2,0},{3,1},{4,6},{5,7},{6,4},{7,5},{8,10},{9,11},{10,... | collective-permute-start | bytes 1572872 | tf_op jit(solution)/shard_map/ppermute | solution.py:219
  18.3 8.9 %collective-permute-start.5 = (bf16[64,2048]{1,0:T(8,128)(2,1)S(1)}, bf16[64,2048]{1,0:T(8,128)(2,1)S(1)}, u32[]{:S(2)}, u32[]{:S(2)}) collective-permute-start(bf16[64,2048]{1,0:T(8,128)(2,1)S(1)} %half.3), channel_id=1, source_target_pairs={{0,2},{1,3},{2,0},{3,1},{4,6},{5,7},{6,4},{7,5},{8,10},{9,11},{10,... | collective-permute-start | bytes 786440 | tf_op jit(solution)/shard_map/ppermute | solution.py:219
  20.1 7.7 %collective-permute-start.4 = (bf16[64,2048]{1,0:T(8,128)(2,1)S(1)}, bf16[64,2048]{1,0:T(8,128)(2,1)S(1)}, u32[]{:S(2)}, u32[]{:S(2)}) collective-permute-start(bf16[64,2048]{1,0:T(8,128)(2,1)S(1)} %half.2), channel_id=1, source_target_pairs={{0,4},{1,5},{2,6},{3,7},{4,0},{5,1},{6,2},{7,3},{8,12},{9,13},{10,... | collective-permute-start | bytes 786440 | tf_op jit(solution)/shard_map/ppermute | solution.py:219
  30.7 6.4 %collective-permute-start.9 = (f32[4,2048]{1,0:T(4,128)S(1)}, f32[4,2048]{1,0:T(4,128)S(1)}, u32[]{:S(2)}, u32[]{:S(2)}) collective-permute-start(f32[4,2048]{1,0:T(4,128)S(1)} %get-tuple-element.93.own_ref), channel_id=1, source_target_pairs={{0,6},{1,7},{2,4},{3,5},{4,2},{5,3},{6,0},{7,1},{8,14},{9,15},{10,... | collective-permute-start | bytes 98312 | tf_op jit(solution)/shard_map/ppermute | solution.py:219
  32.3 4.8 %collective-permute-start.8 = (f32[4,2048]{1,0:T(4,128)S(1)}, f32[4,2048]{1,0:T(4,128)S(1)}, u32[]{:S(2)}, u32[]{:S(2)}) collective-permute-start(f32[4,2048]{1,0:T(4,128)S(1)} %get-tuple-element.93.own_ref), channel_id=1, source_target_pairs={{0,4},{1,5},{2,6},{3,7},{4,0},{5,1},{6,2},{7,3},{8,12},{9,13},{10,... | collective-permute-start | bytes 98312 | tf_op jit(solution)/shard_map/ppermute | solution.py:219
  33.4 3.9 %collective-permute-start.7 = (f32[4,2048]{1,0:T(4,128)S(1)}, f32[4,2048]{1,0:T(4,128)S(1)}, u32[]{:S(2)}, u32[]{:S(2)}) collective-permute-start(f32[4,2048]{1,0:T(4,128)S(1)} %get-tuple-element.93.own_ref), channel_id=1, source_target_pairs={{0,2},{1,3},{2,0},{3,1},{4,6},{5,7},{6,4},{7,5},{8,10},{9,11},{10,... | collective-permute-start | bytes 98312 | tf_op jit(solution)/shard_map/ppermute | solution.py:219
  41.0 10.0 %collective-permute-start.10 = (bf16[1088,128]{1,0:T(8,128)(2,1)S(1)}, bf16[1088,128]{1,0:T(8,128)(2,1)S(1)}, u32[]{:S(2)}, u32[]{:S(2)}) collective-permute-start(bf16[1088,128]{1,0:T(8,128)(2,1)S(1)} %get-tuple-element.124), channel_id=1, source_target_pairs={{0,4},{1,5},{2,6},{3,7},{4,0},{5,1},{6,2},{7,3},{8,12},{9,13},{10,... | collective-permute-start | bytes 835592 | tf_op jit(solution)/shard_map/ppermute | solution.py:219
  42.5 9.6 %collective-permute-start.12 = (bf16[1088,128]{1,0:T(8,128)(2,1)S(1)}, bf16[1088,128]{1,0:T(8,128)(2,1)S(1)}, u32[]{:S(2)}, u32[]{:S(2)}) collective-permute-start(bf16[1088,128]{1,0:T(8,128)(2,1)S(1)} %get-tuple-element.111), channel_id=1, source_target_pairs={{0,2},{1,3},{2,0},{3,1},{4,6},{5,7},{6,4},{7,5},{8,10},{9,11},{10,... | collective-permute-start | bytes 835592 | tf_op jit(solution)/shard_map/ppermute | solution.py:219
  45.7 13.4 %collective-permute-start.14 = (bf16[1056,128]{1,0:T(8,128)(2,1)S(1)}, bf16[1056,128]{1,0:T(8,128)(2,1)S(1)}, u32[]{:S(2)}, u32[]{:S(2)}) collective-permute-start(bf16[1056,128]{1,0:T(8,128)(2,1)S(1)} %get-tuple-element.120), channel_id=1, source_target_pairs={{0,2},{1,3},{2,0},{3,1},{4,6},{5,7},{6,4},{7,5},{8,10},{9,11},{10,... | collective-permute-start | bytes 811016 | tf_op jit(solution)/shard_map/ppermute | solution.py:219
  46.7 12.4 %collective-permute-start.15 = (bf16[1056,128]{1,0:T(8,128)(2,1)S(1)}, bf16[1056,128]{1,0:T(8,128)(2,1)S(1)}, u32[]{:S(2)}, u32[]{:S(2)}) collective-permute-start(bf16[1056,128]{1,0:T(8,128)(2,1)S(1)} %get-tuple-element.140), channel_id=1, source_target_pairs={{0,4},{1,5},{2,6},{3,7},{4,0},{5,1},{6,2},{7,3},{8,12},{9,13},{10,... | collective-permute-start | bytes 811016 | tf_op jit(solution)/shard_map/ppermute | solution.py:219
  47.3 3.7 %collective-permute-start.11 = (f32[1,128]{1,0:T(1,128)S(1)}, f32[1,128]{1,0:T(1,128)S(1)}, u32[]{:S(2)}, u32[]{:S(2)}) collective-permute-start(f32[1,128]{1,0:T(1,128)S(1)} %get-tuple-element.126.first_ref), channel_id=1, source_target_pairs={{0,8},{8,0},{16,24},{24,16},{1,9},{9,1},{17,25},{25,17},{2,10},{10... | collective-permute-start | bytes 1544 | tf_op jit(solution)/shard_map/ppermute | solution.py:837
  52.2 7.7 %collective-permute-start.16 = (bf16[1040,128]{1,0:T(8,128)(2,1)S(1)}, bf16[1040,128]{1,0:T(8,128)(2,1)S(1)}, u32[]{:S(2)}, u32[]{:S(2)}) collective-permute-start(bf16[1040,128]{1,0:T(8,128)(2,1)S(1)} %get-tuple-element.143), channel_id=1, source_target_pairs={{0,2},{1,3},{2,0},{3,1},{4,6},{5,7},{6,4},{7,5},{8,10},{9,11},{10,... | collective-permute-start | bytes 798728 | tf_op jit(solution)/shard_map/ppermute | solution.py:219
  53.2 6.4 %collective-permute-start.17 = (bf16[1024,128]{1,0:T(8,128)(2,1)S(1)}, bf16[1024,128]{1,0:T(8,128)(2,1)S(1)}, u32[]{:S(2)}, u32[]{:S(2)}) collective-permute-start(bf16[1024,128]{1,0:T(8,128)(2,1)S(1)} %get-tuple-element.144), channel_id=1, source_target_pairs={{0,4},{1,5},{2,6},{3,7},{4,0},{5,1},{6,2},{7,3},{8,12},{9,13},{10,... | collective-permute-start | bytes 786440 | tf_op jit(solution)/shard_map/ppermute | solution.py:219
  53.7 4.7 %collective-permute-start.13 = (f32[2,128]{1,0:T(2,128)S(1)}, f32[2,128]{1,0:T(2,128)S(1)}, u32[]{:S(2)}, u32[]{:S(2)}) collective-permute-start(f32[2,128]{1,0:T(2,128)S(1)} %pack.1.near_scores_ref), channel_id=1, source_target_pairs={{0,16},{8,24},{16,0},{24,8},{1,17},{9,25},{17,1},{25,9},{2,18},{10... | collective-permute-start | bytes 3080 | tf_op jit(solution)/shard_map/ppermute | solution.py:854
where the time goes:
time: 61.9 us; the launch traced here: 61.7 us
  Pallas kernels  33.8 us (55%)
  starting transfers between devices  22 us (36%)
  waiting for transfers between devices  4.94 us (8%)
  between operations  0.97 us (2%)
    pallas_call x20, Pallas kernels, kernel_call(): pl.pallas_call(body, name=name, out_shape=outs, in_specs=[pl.BlockSpec(me...  33.8 us
    ppermute x16, starting transfers between devices, swap(): lax.ppermute(value, 'exp', [(index, index ^ bit) for index in range(size)])  17.8 us
    ppermute x16, waiting for transfers between devices, swap(): lax.ppermute(value, 'exp', [(index, index ^ bit) for index in range(size)])  4.94 us
    ppermute x1, starting transfers between devices, every_expert(): lax.ppermute(near_scores, 'psg', [(index, index ^ 2) for index in range(p...  2.59 us
    ppermute x1, starting transfers between devices, every_expert(): lax.ppermute(travelling, 'psg', [(index, index ^ 1) for index in range(pa...  1.58 us
  transfers between devices with their start and end apart: 18, of which 6 were waited for; matrix products, arithmetic and copies ran while one was open for 0% of the time, Pallas kernels for 41%

commit v1 on v0

--- a/solution.py
+++ b/solution.py
@@ -235,9 +235,10 @@
     return pltpu.with_memory_space_constraint(array, pltpu.VMEM)
 
 
-def kernel_call(body, name, outs, ins, far=(), scratch=(), result=pltpu.VMEM):
+def kernel_call(body, name, outs, ins, far=(), scratch=(), result=pltpu.VMEM, earlier=()):
+    aliases = {len(ins) + index: index for index in range(len(earlier))}
+    ins = [*ins, *(pinned(array) for array in earlier)]
     spaces = [pltpu.VMEM] * len(ins)
-    ins = list(ins)
     for index in far:
         spaces[index] = pl.ANY
         ins[index] = pltpu.with_memory_space_constraint(ins[index], pltpu.HBM)
@@ -248,6 +249,7 @@
         in_specs=[pl.BlockSpec(memory_space=space) for space in spaces],
         out_specs=[pl.BlockSpec(memory_space=result)] * len(outs),
         scratch_shapes=scratch,
+        input_output_aliases=aliases,
         compiler_params=pltpu.CompilerParams(vmem_limit_bytes=8 * MIB),
         cost_estimate=pl.CostEstimate(flops=1, bytes_accessed=1, transcendentals=0),
     )(*ins)
@@ -298,6 +300,14 @@
     rows = hidden_ref[...].astype(jnp.float32)
     normed_ref[...] = (rows * rms_scale(rows) * gain_ref[...]).astype(jnp.bfloat16)
     sums_ref[...] = jnp.sum(rows, axis=0, keepdims=True)
+
+
+def on_side(side, body, held, far_count, *refs):
+    refs = refs[:far_count] + refs[far_count + held :]
+
+    @pl.when(lax.rem(lax.axis_index("exp"), 2) == side)
+    def run():
+        body(*refs)
 
 
 def front_kernel(stage, owners, sets, count, router_ref, *refs):
@@ -397,7 +407,7 @@
     terms_ref[...] = (terms + jnp.where(row == 0, sums_ref[...], 0.0))[:4]
 
 
-def front(stage, owners, sets, pieces, router_rows, matrices, more=()):
+def front(stage, owners, sets, pieces, router_rows, matrices, more=(), side=None, earlier=()):
     model_width, hidden_units = matrices[0].shape
     row_total = sum(piece.shape[0] for piece in pieces)
     outs = [kept((row_total, 8), jnp.float32)]
@@ -422,14 +432,11 @@
         matrices = [pinned(matrix) for matrix in matrices]
     if stage == 3:
         more = [pinned(array) for array in more]
-    return kernel_call(
-        functools.partial(front_kernel, stage, owners, sets, len(pieces)),
-        "front",
-        outs,
-        [pinned(router_rows), *matrices, *(pinned(piece) for piece in pieces), *more],
-        far,
-        scratch,
-    )
+    body = functools.partial(front_kernel, stage, owners, sets, len(pieces))
+    ins = [pinned(router_rows), *matrices, *(pinned(piece) for piece in pieces), *more]
+    if side is not None:
+        body = functools.partial(on_side, side, body, len(earlier), len(ins))
+    return kernel_call(body, "front", outs, ins, far, scratch, earlier=earlier)
 
 
 def near_kernel(
@@ -754,22 +761,32 @@
         ],
     )
     others = [swap(matrix, CORE) for matrix in mine]
+    def own_front(side, *earlier):
+        arrays = front(
+            0, (0,), (0,), [normed], router_rows, [gate_matrix, up_matrix], (), side, earlier[:8]
+        )
+        ins = [grades, passage_ranks, down_matrix]
+        body = functools.partial(on_side, side, pair_kernel, len(earlier[8:]), len(ins))
+        pairs = kernel_call(
+            body,
+            "pairs",
+            [kept((8, 128), jnp.float32), kept(down_matrix.shape, jnp.bfloat16)],
+            ins,
+            (0, 1, 2),
+            [
+                pltpu.SMEM(grades.shape, jnp.int32),
+                pltpu.SMEM(grades.shape, jnp.int32),
+                pltpu.SemaphoreType.DMA((3,)),
+            ],
+            earlier=earlier[8:],
+        )
+        return [*arrays, *pairs]
+
+    arrays = own_front(1)
+    normed, *arrays = lax.optimization_barrier((normed, *arrays))
     x_rows, y_rows = swap(normed, ACROSS_X), swap(normed, ACROSS_Y)
-    turned_gates, own_gates, *own_saved, own_part, mine[0], mine[1] = front(
-        0, (0,), (0,), [normed], router_rows, mine[:2]
-    )
-    swap_gain, mine[2] = kernel_call(
-        pair_kernel,
-        "pairs",
-        [kept((8, 128), jnp.float32), kept(down_matrix.shape, jnp.bfloat16)],
-        [grades, after(passage_ranks, own_part), down_matrix],
-        (0, 1, 2),
-        [
-            pltpu.SMEM(grades.shape, jnp.int32),
-            pltpu.SMEM(grades.shape, jnp.int32),
-            pltpu.SemaphoreType.DMA((3,)),
-        ],
-    )
+    arrays = own_front(0, *arrays)
+    turned_gates, own_gates, *own_saved, own_part, mine[0], mine[1], swap_gain, mine[2] = arrays
     *mine_turned, down_turned = turn(mine)
     x_rows, y_rows = after(x_rows, mine_turned[0]), after(y_rows, mine_turned[0])
     far_low = swap(half_of(x_rows, 0), ACROSS_Y)

time: 61.9 us -> 60.9 us (0.984); the launches traced: 61.7 us -> 60 us
  starting transfers between devices: 22 us -> 20 us
    ppermute x16, starting transfers between devices: 17.8 us -> 15.8 us  [swap(): lax.ppermute(value, 'exp', [(index, index ^ bit) for index in range(size)])]
    pallas_call x20 -> x22, Pallas kernels: 33.8 us -> 34 us  [kernel_call(): pl.pallas_call(body, name=name, out_shape=outs, in_specs=[pl.BlockSpec(me...]
  transfers between devices with their start and end apart: 18 -> 18, of which waited for: 6 -> 2; matrix products, arithmetic and copies ran while one was open for 0% -> 0% of each run, Pallas kernels for 41% -> 42%
where the time goes in v1:
time: 60.9 us; the launch traced here: 60 us
  Pallas kernels  34 us (56%)
  starting transfers between devices  20 us (33%)
  waiting for transfers between devices  4.94 us (8%)
  between operations  1.04 us (2%)
    pallas_call x22, Pallas kernels, kernel_call(): pl.pallas_call(body, name=name, out_shape=outs, in_specs=[pl.BlockSpec(me...  34 us
    ppermute x16, starting transfers between devices, swap(): lax.ppermute(value, 'exp', [(index, index ^ bit) for index in range(size)])  15.8 us
    ppermute x16, waiting for transfers between devices, swap(): lax.ppermute(value, 'exp', [(index, index ^ bit) for index in range(size)])  4.93 us
    ppermute x1, starting transfers between devices, every_expert(): lax.ppermute(near_scores, 'psg', [(index, index ^ 2) for index in range(p...  2.59 us
    ppermute x1, starting transfers between devices, every_expert(): lax.ppermute(travelling, 'psg', [(index, index ^ 1) for index in range(pa...  1.58 us
  transfers between devices with their start and end apart: 18, of which 2 were waited for; matrix products, arithmetic and copies ran while one was open for 0% of the time, Pallas kernels for 42%

profile of v1, /device:TPU:0, one launch (start us, length us, event | category | flops | bytes accessed | tf_op | source)
XLA Modules:
  0.0 60.0 jit_solution(774419573441750199)
XLA Ops:
  0.6 0.5 collective-permute-start
  1.2 0.4 collective-permute-start.6
  1.7 1.4 %norm.1 = (bf16[128,2048]{1,0:T(8,128)(2,1)S(1)}, f32[1,2048]{1,0:T(1,128)S(1)}, bf16[8,2048]{1,0:T(8,128)(2,1)S(1)}, bf16[128,2048]{1,0:T(8,128)(2,1)S(1)}, f32...) custom-call(bf16[128,2048]{1,0:T(8,128)(2,1)} %bitcast.19, f32[1,2048]{1,0:T(1,128)} %bitcast.22, bf16[8,2048]{1,0:T(8,128)(2,1)} %bitcast.21, ...), custom_call_target="tpu_custom_call" | custom-call | flops 1 | bytes 1 | tf_op jit(solution)/shard_map/norm/pallas_call | solution.py:245
  3.2 2.7 %collective-permute-start.2 = (bf16[128,2048]{1,0:T(8,128)(2,1)S(1)}, bf16[128,2048]{1,0:T(8,128)(2,1)S(1)}, u32[]{:S(2)}, u32[]{:S(2)}) collective-permute-start(bf16[128,2048]{1,0:T(8,128)(2,1)S(1)} %get-tuple-element.111.refs_3_.refs_2_), channel_id=1, source_target_pairs={{0,4},{1,5},{2,6},{3,7},{4,0},{5,1},{6,2},{7,3},{8,12},{9,13},{10,... | collective-permute-start | bytes 1572872 | tf_op jit(solution)/shard_map/ppermute | solution.py:219
  5.8 1.5 %collective-permute-start.1 = (bf16[128,2048]{1,0:T(8,128)(2,1)S(1)}, bf16[128,2048]{1,0:T(8,128)(2,1)S(1)}, u32[]{:S(2)}, u32[]{:S(2)}) collective-permute-start(bf16[128,2048]{1,0:T(8,128)(2,1)S(1)} %get-tuple-element.111.refs_3_.refs_2_), channel_id=1, source_target_pairs={{0,2},{1,3},{2,0},{3,1},{4,6},{5,7},{6,4},{7,5},{8,10},{9,11},{10,... | collective-permute-start | bytes 1572872 | tf_op jit(solution)/shard_map/ppermute | solution.py:219
  7.3 1.9 %pairs.3 = (f32[8,128]{1,0:T(8,128)S(1)}, bf16[768,2048]{1,0:T(8,128)(2,1)S(1)}) custom-call(s32[1,4]{1,0:T(1,128)} %refs_0_.3, s32[1,4]{1,0:T(1,128)} %refs_1_.3, bf16[768,2048]{1,0:T(8,128)(2,1)} %bitcast.12, f32[8,128]{1,0:T(8,128)S(1)} %get-tuple-element.108.refs_3_, ...), custom_call_target="tpu_custom_call", output_to_operand_aliasing={{0}: (3, {}), {1}: (4, {})} | custom-call | flops 1 | bytes 1 | tf_op jit(solution)/shard_map/pairs/pallas_call | solution.py:245
  9.3 3.7 %front.6 = (f32[8,128]{1,0:T(8,128)S(1)}, f32[128,8]{1,0:T(8,128)S(1)}, f32[128,768]{1,0:T(8,128)S(1)}, f32[128,768]{1,0:T(8,128)S(1)}, bf16[128,768]{1,0:T(8,12...) custom-call(bf16[8,2048]{1,0:T(8,128)(2,1)S(1)} %get-tuple-element.9, ...), custom_call_target="tpu_custom_call", output_to_operand_aliasing={{0}: (4, {}), {1}: (5, {}), {2}: (6, {}), {3}: (7, {}), {4}... | custom-call | flops 1 | bytes 1 | tf_op jit(solution)/shard_map/front/pallas_call | solution.py:245
  13.0 2.6 %turn.2 = (bf16[768,2048]{1,0:T(8,128)(2,1)S(1)}, bf16[768,2048]{1,0:T(8,128)(2,1)S(1)}, bf16[2048,768]{1,0:T(8,128)(2,1)S(1)}) custom-call(bf16[2048,768]{1,0:T(8,128)(2,1)S(1)} %get-tuple-element.120.refs_0_, bf16[2048,768]{1,0:T(8,128)(2,1)S(1)} %get-tuple-element.121.refs_1_, bf16[768,2048]{1,0:T(8,128)(2,1)S(1)} %get-tuple-element.122.refs_2_.refs_7_), custom_call_target="tpu_custom_call" | custom-call | flops 1 | bytes 1 | tf_op jit(solution)/shard_map/turn/pallas_call | solution.py:245
  15.7 0.6 collective-permute-start.5
  16.3 1.0 %collective-permute-start.4 = (bf16[64,2048]{1,0:T(8,128)(2,1)S(1)}, bf16[64,2048]{1,0:T(8,128)(2,1)S(1)}, u32[]{:S(2)}, u32[]{:S(2)}) collective-permute-start(bf16[64,2048]{1,0:T(8,128)(2,1)S(1)} %half.2), channel_id=1, source_target_pairs={{0,4},{1,5},{2,6},{3,7},{4,0},{5,1},{6,2},{7,3},{8,12},{9,13},{10,... | collective-permute-start | bytes 786440 | tf_op jit(solution)/shard_map/ppermute | solution.py:219
  17.3 2.1 %front.7 = (f32[256,8]{1,0:T(8,128)S(1)}, f32[256,768]{1,0:T(8,128)S(1)}, f32[256,768]{1,0:T(8,128)S(1)}, bf16[256,768]{1,0:T(8,128)(2,1)S(1)}, f32[8,768]{1,0:T(8,128)S(1)}) custom-call(bf16[8,2048]{1,0:T(8,128)(2,1)S(1)} %get-tuple-element.97.refs_0_.router_ref, bf16[2048,768]{1,0:T(8,128)(2,1)S(1)} %get-tuple-element.120.refs_0_, ...), custom_call_target="tpu_custom_call" | custom-call | flops 1 | bytes 1 | tf_op jit(solution)/shard_map/front/pallas_call | solution.py:245
  19.4 3.4 %front.8 = (f32[384,8]{1,0:T(8,128)}, f32[384,768]{1,0:T(8,128)S(1)}, f32[384,768]{1,0:T(8,128)S(1)}, bf16[384,768]{1,0:T(8,128)(2,1)S(1)}, f32[8,768]{1,0:T(8,128)S(1)}) custom-call(bf16[8,2048]{1,0:T(8,128)(2,1)S(1)} %get-tuple-element.97.refs_0_.router_ref, bf16[2048,768]{1,0:T(8,128)(2,1)S(1)} %collective-permute-done.refs_0_.refs_2_, ...), custom_call_target="tpu_custom_call" | custom-call | flops 1 | bytes 1 | tf_op jit(solution)/shard_map/front/pallas_call | solution.py:245
  22.8 2.2 %collective-permute-done.5.refs_5_ = bf16[64,2048]{1,0:T(8,128)(2,1)S(1)} collective-permute-done((bf16[64,2048]{1,0:T(8,128)(2,1)S(1)}, bf16[64,2048]{1,0:T(8,128)(2,1)S(1)}, u32[]{:S(2)}, u32[]{:S(2)}) %collective-permute-start.5) | collective-permute-done | bytes 262176 | tf_op jit(solution)/shard_map/ppermute | solution.py:219
  25.0 3.0 %front.9 = (f32[128,8]{1,0:T(8,128)S(1)}, f32[128,768]{1,0:T(8,128)S(1)}, f32[128,768]{1,0:T(8,128)S(1)}, bf16[128,768]{1,0:T(8,128)(2,1)S(1)}, f32[128,768]{1,0...) custom-call(bf16[8,2048]{1,0:T(8,128)(2,1)S(1)} %get-tuple-element.97.refs_0_.router_ref,, ...), custom_call_target="tpu_custom_call" | custom-call | flops 1 | bytes 1 | tf_op jit(solution)/shard_map/front/pallas_call | solution.py:245
  28.3 1.8 %collective-permute-start.8 = (f32[4,2048]{1,0:T(4,128)S(1)}, f32[4,2048]{1,0:T(4,128)S(1)}, u32[]{:S(2)}, u32[]{:S(2)}) collective-permute-start(f32[4,2048]{1,0:T(4,128)S(1)} %get-tuple-element.133.own_ref), channel_id=1, source_target_pairs={{0,4},{1,5},{2,6},{3,7},{4,0},{5,1},{6,2},{7,3},{8,12},{9,13},{10,... | collective-permute-start | bytes 98312 | tf_op jit(solution)/shard_map/ppermute | solution.py:219
  30.1 1.5 %collective-permute-start.7 = (f32[4,2048]{1,0:T(4,128)S(1)}, f32[4,2048]{1,0:T(4,128)S(1)}, u32[]{:S(2)}, u32[]{:S(2)}) collective-permute-start(f32[4,2048]{1,0:T(4,128)S(1)} %get-tuple-element.133.own_ref), channel_id=1, source_target_pairs={{0,2},{1,3},{2,0},{3,1},{4,6},{5,7},{6,4},{7,5},{8,10},{9,11},{10,... | collective-permute-start | bytes 98312 | tf_op jit(solution)/shard_map/ppermute | solution.py:219
  31.6 2.6 %turn.3 = (bf16[768,2048]{1,0:T(8,128)(2,1)S(1)}, bf16[768,2048]{1,0:T(8,128)(2,1)S(1)}, bf16[2048,768]{1,0:T(8,128)(2,1)S(1)}) custom-call(bf16[2048,768]{1,0:T(8,128)(2,1)S(1)} %collective-permute-done.refs_0_.refs_2_, bf16[2048,768]{1,0:T(8,128)(2,1)S(1)} %collective-permute-done.3.refs_1_.refs_3_, ...), custom_call_target="tpu_custom_call" | custom-call | flops 1 | bytes 1 | tf_op jit(solution)/shard_map/turn/pallas_call | solution.py:245
  34.3 1.7 %near.1 = (f32[8,768]{1,0:T(8,128)S(1)}, f32[8,768]{1,0:T(8,128)S(1)}, f32[1,2048]{1,0:T(1,128)S(1)}, f32[1,128]{1,0:T(1,128)S(1)}, f32[1,1]{1,0:T(1,128)}) custom-call(f32[4,2048]{1,0:T(4,128)S(1)} %get-tuple-element.133.own_ref, f32[4,2048]{1,0:T(4,128)S(1)} %collective-permute-done.7.x_ref, f32[4,2048]{1,0:T(4,128)S(1)} %collective-permute-done.8.y_ref, ...), custom_call_target="tpu_custom_call" | custom-call | flops 1 | bytes 1 | tf_op jit(solution)/shard_map/near/pallas_call | solution.py:245
  36.0 2.3 %back.4 = (bf16[1088,128]{1,0:T(8,128)(2,1)S(1)}, bf16[1088,128]{1,0:T(8,128)(2,1)S(1)}) custom-call(f32[8,768]{1,0:T(8,128)S(1)} %get-tuple-element.161.near_ref, f32[8,768]{1,0:T(8,128)S(1)} %get-tuple-element.174.other_near_ref, f32[128,8]{1,0:T(8,128)S(1)} %get-tuple-element.142.refs_0_, f32[128,768]{1,0:T(8,128)S(1)} %get-tuple-element.143.refs_1_, ...), custom_call_target="tpu_custom_call" | custom-call | flops 1 | bytes 1 | tf_op jit(solution)/shard_map/back/pallas_call | solution.py:245
  38.3 1.3 %collective-permute-start.12 = (bf16[1088,128]{1,0:T(8,128)(2,1)S(1)}, bf16[1088,128]{1,0:T(8,128)(2,1)S(1)}, u32[]{:S(2)}, u32[]{:S(2)}) collective-permute-start(bf16[1088,128]{1,0:T(8,128)(2,1)S(1)} %get-tuple-element.151), channel_id=1, source_target_pairs={{0,2},{1,3},{2,0},{3,1},{4,6},{5,7},{6,4},{7,5},{8,10},{9,11},{10,... | collective-permute-start | bytes 835592 | tf_op jit(solution)/shard_map/ppermute | solution.py:219
  39.6 2.1 %back.5 = (bf16[1056,128]{1,0:T(8,128)(2,1)S(1)}, bf16[1056,128]{1,0:T(8,128)(2,1)S(1)}) custom-call(f32[8,768]{1,0:T(8,128)S(1)} %get-tuple-element.161.near_ref, f32[8,768]{1,0:T(8,128)S(1)} %get-tuple-element.174.other_near_ref, f32[256,8]{1,0:T(8,128)S(1)} %get-tuple-element.153.refs_0_, f32[256,768]{1,0:T(8,128)S(1)} %get-tuple-element.154.refs_1_, ...), custom_call_target="tpu_custom_call" | custom-call | flops 1 | bytes 1 | tf_op jit(solution)/shard_map/back/pallas_call | solution.py:245
  41.7 0.9 %collective-permute-start.14 = (bf16[1056,128]{1,0:T(8,128)(2,1)S(1)}, bf16[1056,128]{1,0:T(8,128)(2,1)S(1)}, u32[]{:S(2)}, u32[]{:S(2)}) collective-permute-start(bf16[1056,128]{1,0:T(8,128)(2,1)S(1)} %get-tuple-element.160), channel_id=1, source_target_pairs={{0,2},{1,3},{2,0},{3,1},{4,6},{5,7},{6,4},{7,5},{8,10},{9,11},{10,... | collective-permute-start | bytes 811016 | tf_op jit(solution)/shard_map/ppermute | solution.py:219
  42.6 1.9 %collective-permute-start.15 = (bf16[1056,128]{1,0:T(8,128)(2,1)S(1)}, bf16[1056,128]{1,0:T(8,128)(2,1)S(1)}, u32[]{:S(2)}, u32[]{:S(2)}) collective-permute-start(bf16[1056,128]{1,0:T(8,128)(2,1)S(1)} %get-tuple-element.180), channel_id=1, source_target_pairs={{0,4},{1,5},{2,6},{3,7},{4,0},{5,1},{6,2},{7,3},{8,12},{9,13},{10,... | collective-permute-start | bytes 811016 | tf_op jit(solution)/shard_map/ppermute | solution.py:219
  44.5 1.6 %collective-permute-start.11 = (f32[1,128]{1,0:T(1,128)S(1)}, f32[1,128]{1,0:T(1,128)S(1)}, u32[]{:S(2)}, u32[]{:S(2)}) collective-permute-start(f32[1,128]{1,0:T(1,128)S(1)} %get-tuple-element.166.first_ref), channel_id=1, source_target_pairs={{0,8},{8,0},{16,24},{24,16},{1,9},{9,1},{17,25},{25,17},{2,10},{10... | collective-permute-start | bytes 1544 | tf_op jit(solution)/shard_map/ppermute | solution.py:854
  46.1 2.1 %back.6 = (bf16[1040,128]{1,0:T(8,128)(2,1)S(1)}, bf16[1024,128]{1,0:T(8,128)(2,1)S(1)}) custom-call(f32[8,768]{1,0:T(8,128)S(1)} %get-tuple-element.161.near_ref, f32[8,768]{1,0:T(8,128)S(1)} %get-tuple-element.174.other_near_ref, f32[256,8]{1,0:T(8,128)S(1)} %get-tuple-element.153.refs_0_, f32[256,768]{1,0:T(8,128)S(1)} %get-tuple-element.154.refs_1_, ...), custom_call_target="tpu_custom_call" | custom-call | flops 1 | bytes 1 | tf_op jit(solution)/shard_map/back/pallas_call | solution.py:245
  48.4 1.3 %collective-permute-start.16 = (bf16[1040,128]{1,0:T(8,128)(2,1)S(1)}, bf16[1040,128]{1,0:T(8,128)(2,1)S(1)}, u32[]{:S(2)}, u32[]{:S(2)}) collective-permute-start(bf16[1040,128]{1,0:T(8,128)(2,1)S(1)} %get-tuple-element.183), channel_id=1, source_target_pairs={{0,2},{1,3},{2,0},{3,1},{4,6},{5,7},{6,4},{7,5},{8,10},{9,11},{10,... | collective-permute-start | bytes 798728 | tf_op jit(solution)/shard_map/ppermute | solution.py:219
  49.8 2.6 %collective-permute-start.13 = (f32[2,128]{1,0:T(2,128)S(1)}, f32[2,128]{1,0:T(2,128)S(1)}, u32[]{:S(2)}, u32[]{:S(2)}) collective-permute-start(f32[2,128]{1,0:T(2,128)S(1)} %pack.1.near_scores_ref), channel_id=1, source_target_pairs={{0,16},{8,24},{16,0},{24,8},{1,17},{9,25},{17,1},{25,9},{2,18},{10... | collective-permute-start | bytes 3080 | tf_op jit(solution)/shard_map/ppermute | solution.py:871
  52.3 2.1 %back.7.own_ref = bf16[2064,128]{1,0:T(8,128)(2,1)S(1)} custom-call(f32[8,768]{1,0:T(8,128)S(1)} %get-tuple-element.161.near_ref, f32[8,768]{1,0:T(8,128)S(1)} %get-tuple-element.174.other_near_ref, f32[128,8]{1,0:T(8,128)S(1)} %get-tuple-element.175.refs_0_, f32[128,768]{1,0:T(8,128)S(1)} %get-tuple-element.176.refs_1_, ...), custom_call_target="tpu_custom_call" | custom-call | flops 1 | bytes 1 | tf_op jit(solution)/shard_map/back/pallas_call | solution.py:245
  54.4 0.6 %rank.1 = (f32[1,1]{1,0:T(1,128)}, f32[1,128]{1,0:T(1,128)S(1)}) custom-call(f32[8,128]{1,0:T(8,128)S(1)} %get-tuple-element.110.swap_gain_ref, f32[2,128]{1,0:T(2,128)S(1)} %pack.1.near_scores_ref, f32[2,128]{1,0:T(2,128)S(1)} %collective-permute-done.13.far_scores_ref), custom_call_target="tpu_custom_call" | custom-call | flops 1 | bytes 1 | tf_op jit(solution)/shard_map/rank/pallas_call | solution.py:245
  55.1 0.3 first_end.1
  55.4 2.7 %collective-permute-done.17.y_low_ref = bf16[1024,128]{1,0:T(8,128)(2,1)S(1)} collective-permute-done((bf16[1024,128]{1,0:T(8,128)(2,1)S(1)}, bf16[1024,128]{1,0:T(8,128)(2,1)S(1)}, u32[]{:S(2)}, u32[]{:S(2)}) %collective-permute-start.17) | collective-permute-done | bytes 262176 | tf_op jit(solution)/shard_map/ppermute | solution.py:219
  58.1 1.7 %end.1 = bf16[128,2048]{1,0:T(8,128)(2,1)} custom-call(f32[1,128]{1,0:T(1,128)S(1)} %get-tuple-element.173.factor_ref, f32[128,2048]{1,0:T(8,128)S(1)} %get-tuple-element.181.total_ref, f32[8,128]{1,0:T(8,128)S(1)} %get-tuple-element.182.lines_ref, bf16[1040,128]{1,0:T(8,128)(2,1)S(1)} %collective-permute-done.16.x_high_ref, ...), custom_call_target="tpu_custom_call" | custom-call | flops 1 | bytes 1 | tf_op jit(solution)/shard_map/end/pallas_call | solution.py:245
  (26 shorter events, 0.8 us)
Async XLA Ops:
  0.6 18.8 %collective-permute-start = (bf16[2048,768]{1,0:T(8,128)(2,1)}, bf16[2048,768]{1,0:T(8,128)(2,1)S(1)}, u32[]{:S(2)}, u32[]{:S(2)}) collective-permute-start(bf16[2048,768]{1,0:T(8,128)(2,1)} %bitcast.13), channel_id=1, source_target_pairs={{0,1},{1,0},{2,3},{3,2},{4,5},{5,4},{6,7},{7,6},{8,9},{9,8},{10,11... | collective-permute-start | bytes 9437192 | tf_op jit(solution)/shard_map/ppermute | solution.py:219
  1.1 18.3 %collective-permute-start.3 = (bf16[2048,768]{1,0:T(8,128)(2,1)}, bf16[2048,768]{1,0:T(8,128)(2,1)S(1)}, u32[]{:S(2)}, u32[]{:S(2)}) collective-permute-start(bf16[2048,768]{1,0:T(8,128)(2,1)} %bitcast.16), channel_id=1, source_target_pairs={{0,1},{1,0},{2,3},{3,2},{4,5},{5,4},{6,7},{7,6},{8,9},{9,8},{10,11... | collective-permute-start | bytes 9437192 | tf_op jit(solution)/shard_map/ppermute | solution.py:219
  1.2 23.8 %collective-permute-start.6 = (bf16[768,2048]{1,0:T(8,128)(2,1)}, bf16[768,2048]{1,0:T(8,128)(2,1)S(1)}, u32[]{:S(2)}, u32[]{:S(2)}) collective-permute-start(bf16[768,2048]{1,0:T(8,128)(2,1)} %bitcast.10), channel_id=1, source_target_pairs={{0,1},{1,0},{2,3},{3,2},{4,5},{5,4},{6,7},{7,6},{8,9},{9,8},{10,11... | collective-permute-start | bytes 9437192 | tf_op jit(solution)/shard_map/ppermute | solution.py:219
  3.2 12.5 %collective-permute-start.2 = (bf16[128,2048]{1,0:T(8,128)(2,1)S(1)}, bf16[128,2048]{1,0:T(8,128)(2,1)S(1)}, u32[]{:S(2)}, u32[]{:S(2)}) collective-permute-start(bf16[128,2048]{1,0:T(8,128)(2,1)S(1)} %get-tuple-element.111.refs_3_.refs_2_), channel_id=1, source_target_pairs={{0,4},{1,5},{2,6},{3,7},{4,0},{5,1},{6,2},{7,3},{8,12},{9,13},{10,... | collective-permute-start | bytes 1572872 | tf_op jit(solution)/shard_map/ppermute | solution.py:219
  5.8 10.5 %collective-permute-start.1 = (bf16[128,2048]{1,0:T(8,128)(2,1)S(1)}, bf16[128,2048]{1,0:T(8,128)(2,1)S(1)}, u32[]{:S(2)}, u32[]{:S(2)}) collective-permute-start(bf16[128,2048]{1,0:T(8,128)(2,1)S(1)} %get-tuple-element.111.refs_3_.refs_2_), channel_id=1, source_target_pairs={{0,2},{1,3},{2,0},{3,1},{4,6},{5,7},{6,4},{7,5},{8,10},{9,11},{10,... | collective-permute-start | bytes 1572872 | tf_op jit(solution)/shard_map/ppermute | solution.py:219
  15.7 9.3 %collective-permute-start.5 = (bf16[64,2048]{1,0:T(8,128)(2,1)S(1)}, bf16[64,2048]{1,0:T(8,128)(2,1)S(1)}, u32[]{:S(2)}, u32[]{:S(2)}) collective-permute-start(bf16[64,2048]{1,0:T(8,128)(2,1)S(1)} %half.3), channel_id=1, source_target_pairs={{0,2},{1,3},{2,0},{3,1},{4,6},{5,7},{6,4},{7,5},{8,10},{9,11},{10,... | collective-permute-start | bytes 786440 | tf_op jit(solution)/shard_map/ppermute | solution.py:219
  16.3 8.7 %collective-permute-start.4 = (bf16[64,2048]{1,0:T(8,128)(2,1)S(1)}, bf16[64,2048]{1,0:T(8,128)(2,1)S(1)}, u32[]{:S(2)}, u32[]{:S(2)}) collective-permute-start(bf16[64,2048]{1,0:T(8,128)(2,1)S(1)} %half.2), channel_id=1, source_target_pairs={{0,4},{1,5},{2,6},{3,7},{4,0},{5,1},{6,2},{7,3},{8,12},{9,13},{10,... | collective-permute-start | bytes 786440 | tf_op jit(solution)/shard_map/ppermute | solution.py:219
  28.0 6.2 %collective-permute-start.9 = (f32[4,2048]{1,0:T(4,128)S(1)}, f32[4,2048]{1,0:T(4,128)S(1)}, u32[]{:S(2)}, u32[]{:S(2)}) collective-permute-start(f32[4,2048]{1,0:T(4,128)S(1)} %get-tuple-element.133.own_ref), channel_id=1, source_target_pairs={{0,6},{1,7},{2,4},{3,5},{4,2},{5,3},{6,0},{7,1},{8,14},{9,15},{10,... | collective-permute-start | bytes 98312 | tf_op jit(solution)/shard_map/ppermute | solution.py:219
  28.3 5.9 %collective-permute-start.8 = (f32[4,2048]{1,0:T(4,128)S(1)}, f32[4,2048]{1,0:T(4,128)S(1)}, u32[]{:S(2)}, u32[]{:S(2)}) collective-permute-start(f32[4,2048]{1,0:T(4,128)S(1)} %get-tuple-element.133.own_ref), channel_id=1, source_target_pairs={{0,4},{1,5},{2,6},{3,7},{4,0},{5,1},{6,2},{7,3},{8,12},{9,13},{10,... | collective-permute-start | bytes 98312 | tf_op jit(solution)/shard_map/ppermute | solution.py:219
  30.1 4.2 %collective-permute-start.7 = (f32[4,2048]{1,0:T(4,128)S(1)}, f32[4,2048]{1,0:T(4,128)S(1)}, u32[]{:S(2)}, u32[]{:S(2)}) collective-permute-start(f32[4,2048]{1,0:T(4,128)S(1)} %get-tuple-element.133.own_ref), channel_id=1, source_target_pairs={{0,2},{1,3},{2,0},{3,1},{4,6},{5,7},{6,4},{7,5},{8,10},{9,11},{10,... | collective-permute-start | bytes 98312 | tf_op jit(solution)/shard_map/ppermute | solution.py:219
  38.2 10.0 %collective-permute-start.10 = (bf16[1088,128]{1,0:T(8,128)(2,1)S(1)}, bf16[1088,128]{1,0:T(8,128)(2,1)S(1)}, u32[]{:S(2)}, u32[]{:S(2)}) collective-permute-start(bf16[1088,128]{1,0:T(8,128)(2,1)S(1)} %get-tuple-element.164), channel_id=1, source_target_pairs={{0,4},{1,5},{2,6},{3,7},{4,0},{5,1},{6,2},{7,3},{8,12},{9,13},{10,... | collective-permute-start | bytes 835592 | tf_op jit(solution)/shard_map/ppermute | solution.py:219
  38.3 9.9 %collective-permute-start.12 = (bf16[1088,128]{1,0:T(8,128)(2,1)S(1)}, bf16[1088,128]{1,0:T(8,128)(2,1)S(1)}, u32[]{:S(2)}, u32[]{:S(2)}) collective-permute-start(bf16[1088,128]{1,0:T(8,128)(2,1)S(1)} %get-tuple-element.151), channel_id=1, source_target_pairs={{0,2},{1,3},{2,0},{3,1},{4,6},{5,7},{6,4},{7,5},{8,10},{9,11},{10,... | collective-permute-start | bytes 835592 | tf_op jit(solution)/shard_map/ppermute | solution.py:219
  41.7 13.3 %collective-permute-start.14 = (bf16[1056,128]{1,0:T(8,128)(2,1)S(1)}, bf16[1056,128]{1,0:T(8,128)(2,1)S(1)}, u32[]{:S(2)}, u32[]{:S(2)}) collective-permute-start(bf16[1056,128]{1,0:T(8,128)(2,1)S(1)} %get-tuple-element.160), channel_id=1, source_target_pairs={{0,2},{1,3},{2,0},{3,1},{4,6},{5,7},{6,4},{7,5},{8,10},{9,11},{10,... | collective-permute-start | bytes 811016 | tf_op jit(solution)/shard_map/ppermute | solution.py:219
  42.6 12.5 %collective-permute-start.15 = (bf16[1056,128]{1,0:T(8,128)(2,1)S(1)}, bf16[1056,128]{1,0:T(8,128)(2,1)S(1)}, u32[]{:S(2)}, u32[]{:S(2)}) collective-permute-start(bf16[1056,128]{1,0:T(8,128)(2,1)S(1)} %get-tuple-element.180), channel_id=1, source_target_pairs={{0,4},{1,5},{2,6},{3,7},{4,0},{5,1},{6,2},{7,3},{8,12},{9,13},{10,... | collective-permute-start | bytes 811016 | tf_op jit(solution)/shard_map/ppermute | solution.py:219
  44.5 3.7 %collective-permute-start.11 = (f32[1,128]{1,0:T(1,128)S(1)}, f32[1,128]{1,0:T(1,128)S(1)}, u32[]{:S(2)}, u32[]{:S(2)}) collective-permute-start(f32[1,128]{1,0:T(1,128)S(1)} %get-tuple-element.166.first_ref), channel_id=1, source_target_pairs={{0,8},{8,0},{16,24},{24,16},{1,9},{9,1},{17,25},{25,17},{2,10},{10... | collective-permute-start | bytes 1544 | tf_op jit(solution)/shard_map/ppermute | solution.py:854
  48.4 9.7 %collective-permute-start.16 = (bf16[1040,128]{1,0:T(8,128)(2,1)S(1)}, bf16[1040,128]{1,0:T(8,128)(2,1)S(1)}, u32[]{:S(2)}, u32[]{:S(2)}) collective-permute-start(bf16[1040,128]{1,0:T(8,128)(2,1)S(1)} %get-tuple-element.183), channel_id=1, source_target_pairs={{0,2},{1,3},{2,0},{3,1},{4,6},{5,7},{6,4},{7,5},{8,10},{9,11},{10,... | collective-permute-start | bytes 798728 | tf_op jit(solution)/shard_map/ppermute | solution.py:219
  49.7 8.4 %collective-permute-start.17 = (bf16[1024,128]{1,0:T(8,128)(2,1)S(1)}, bf16[1024,128]{1,0:T(8,128)(2,1)S(1)}, u32[]{:S(2)}, u32[]{:S(2)}) collective-permute-start(bf16[1024,128]{1,0:T(8,128)(2,1)S(1)} %get-tuple-element.184), channel_id=1, source_target_pairs={{0,4},{1,5},{2,6},{3,7},{4,0},{5,1},{6,2},{7,3},{8,12},{9,13},{10,... | collective-permute-start | bytes 786440 | tf_op jit(solution)/shard_map/ppermute | solution.py:219
  49.8 4.7 %collective-permute-start.13 = (f32[2,128]{1,0:T(2,128)S(1)}, f32[2,128]{1,0:T(2,128)S(1)}, u32[]{:S(2)}, u32[]{:S(2)}) collective-permute-start(f32[2,128]{1,0:T(2,128)S(1)} %pack.1.near_scores_ref), channel_id=1, source_target_pairs={{0,16},{8,24},{16,0},{24,8},{1,17},{9,25},{17,1},{25,9},{2,18},{10... | collective-permute-start | bytes 3080 | tf_op jit(solution)/shard_map/ppermute | solution.py:871

commit v2 on v0

--- a/solution.py
+++ b/solution.py
@@ -235,9 +235,10 @@
     return pltpu.with_memory_space_constraint(array, pltpu.VMEM)
 
 
-def kernel_call(body, name, outs, ins, far=(), scratch=(), result=pltpu.VMEM):
+def kernel_call(body, name, outs, ins, far=(), scratch=(), result=pltpu.VMEM, earlier=()):
+    aliases = {len(ins) + index: index for index in range(len(earlier))}
+    ins = [*ins, *(pinned(array) for array in earlier)]
     spaces = [pltpu.VMEM] * len(ins)
-    ins = list(ins)
     for index in far:
         spaces[index] = pl.ANY
         ins[index] = pltpu.with_memory_space_constraint(ins[index], pltpu.HBM)
@@ -248,6 +249,7 @@
         in_specs=[pl.BlockSpec(memory_space=space) for space in spaces],
         out_specs=[pl.BlockSpec(memory_space=result)] * len(outs),
         scratch_shapes=scratch,
+        input_output_aliases=aliases,
         compiler_params=pltpu.CompilerParams(vmem_limit_bytes=8 * MIB),
         cost_estimate=pl.CostEstimate(flops=1, bytes_accessed=1, transcendentals=0),
     )(*ins)
@@ -300,6 +302,14 @@
     sums_ref[...] = jnp.sum(rows, axis=0, keepdims=True)
 
 
+def on_side(side, body, held, far_count, *refs):
+    refs = refs[:far_count] + refs[far_count + held :]
+
+    @pl.when(lax.rem(lax.axis_index("exp"), 2) == side)
+    def run():
+        body(*refs)
+
+
 def front_kernel(stage, owners, sets, count, router_ref, *refs):
     matrices, refs = refs[: 2 * len(sets)], refs[2 * len(sets) :]
     pieces, refs = refs[:count], refs[count:]
@@ -307,23 +317,7 @@
     hidden_units = matrices[0].shape[1]
     tile = 256
     firsts = range(0, hidden_units, tile)
-    if stage == 0:
-        far_matrices = matrices
-        *refs, gate_held, up_held, rows_ref, copy_sems = refs
-        matrices = [gate_held, up_held]
-        copies = [
-            pltpu.make_async_copy(
-                source.at[:, first : first + tile],
-                target.at[:, first : first + tile],
-                copy_sems.at[which, number],
-            )
-            for number, first in enumerate(firsts)
-            for which, (source, target) in enumerate(zip(far_matrices, matrices))
-        ]
-        for copy in copies:
-            copy.start()
-        turned_ref, *refs = refs
-    elif stage == 3:
+    if stage == 3:
         sums_ref, *downs = refs[:3]
         earlier, refs = refs[3:6], refs[6:]
         *refs, terms_ref, rows_ref = refs
@@ -343,13 +337,6 @@
     gates = weights / jnp.sum(weights, axis=1, keepdims=True)
     gates_ref[...] = gates
     lane = lax.broadcasted_iota(jnp.int32, gates.shape, 1)
-    if stage == 0:
-        weights = jnp.exp(
-            lax.dot_general(
-                router_ref[...], rows_ref[...], across, preferred_element_type=jnp.float32
-            )
-        )
-        turned_ref[...] = weights / jnp.sum(weights, axis=0, keepdims=True)
 
     totals = []
     for place, which in enumerate(sets):
@@ -361,11 +348,8 @@
         own = jnp.sum(jnp.where(lane == expert ^ which, gates, 0.0), axis=1, keepdims=True)
         low = own.astype(jnp.bfloat16).astype(jnp.float32)
         parts = []
-        for number, first in enumerate(firsts):
+        for first in firsts:
             columns = slice(first, first + tile)
-            if stage == 0:
-                copies[2 * number].wait()
-                copies[2 * number + 1].wait()
             rows = rows_ref[...]
             pre_gate = jnp.dot(rows, gate_ref[:, columns], preferred_element_type=jnp.float32)
             pre_up = jnp.dot(rows, up_ref[:, columns], preferred_element_type=jnp.float32)
@@ -401,8 +385,6 @@
     model_width, hidden_units = matrices[0].shape
     row_total = sum(piece.shape[0] for piece in pieces)
     outs = [kept((row_total, 8), jnp.float32)]
-    if stage == 0:
-        outs.insert(0, kept((8, row_total), jnp.float32))
     for which in sets:
         outs += [
             kept((row_total, hidden_units), jnp.float32),
@@ -413,13 +395,7 @@
         kept((4, model_width), jnp.float32) if stage == 3 else kept((8, hidden_units), jnp.float32)
     )
     scratch = [pltpu.VMEM((row_total, model_width), jnp.bfloat16)]
-    far = ()
-    if stage == 0:
-        far = (1, 2)
-        outs += [kept(matrix.shape, jnp.bfloat16) for matrix in matrices]
-        scratch.append(pltpu.SemaphoreType.DMA((2, hidden_units // 256)))
-    else:
-        matrices = [pinned(matrix) for matrix in matrices]
+    matrices = [pinned(matrix) for matrix in matrices]
     if stage == 3:
         more = [pinned(array) for array in more]
     return kernel_call(
@@ -427,8 +403,107 @@
         "front",
         outs,
         [pinned(router_rows), *matrices, *(pinned(piece) for piece in pieces), *more],
-        far,
+        (),
         scratch,
+    )
+
+
+def turn_block(source_ref, target_ref, rows, columns):
+    target_ref[columns, rows] = source_ref[rows, columns].T
+
+
+def own_kernel(
+    grades_far, ranks_far, gate_far, up_far, down_far, router_ref, rows_ref,
+    turned_ref, gates_ref, slope_ref, silu_ref, act_ref, part_ref, swap_gain_ref,
+    gate_ref, up_ref, down_ref, gate_turned_ref, up_turned_ref, down_turned_ref,
+    grades_ref, ranks_ref, copy_sems,
+):
+    hidden_units = gate_ref.shape[1]
+    model_width = gate_ref.shape[0]
+    tile = 256
+    pairs = [(grades_far, grades_ref), (ranks_far, ranks_ref)]
+    for first in range(0, hidden_units, tile):
+        columns = slice(first, first + tile)
+        pairs += [
+            (gate_far.at[:, columns], gate_ref.at[:, columns]),
+            (up_far.at[:, columns], up_ref.at[:, columns]),
+        ]
+    pairs.append((down_far, down_ref))
+    copies = [
+        pltpu.make_async_copy(source, target, copy_sems.at[index])
+        for index, (source, target) in enumerate(pairs)
+    ]
+    for copy in copies:
+        copy.start()
+    rows = rows_ref[...]
+    weights = jnp.exp(
+        lax.dot_general(rows, router_ref[...], across, preferred_element_type=jnp.float32)
+    )
+    gates = weights / jnp.sum(weights, axis=1, keepdims=True)
+    gates_ref[...] = gates
+    weights = jnp.exp(
+        lax.dot_general(router_ref[...], rows, across, preferred_element_type=jnp.float32)
+    )
+    turned_ref[...] = weights / jnp.sum(weights, axis=0, keepdims=True)
+    lane = lax.broadcasted_iota(jnp.int32, gates.shape, 1)
+    own = jnp.sum(
+        jnp.where(lane == lax.axis_index("exp"), gates, 0.0), axis=1, keepdims=True
+    )
+    low = own.astype(jnp.bfloat16).astype(jnp.float32)
+    copies[0].wait()
+    copies[1].wait()
+    swap_gain_ref[...] = swap_gains(grades_ref, ranks_ref)
+    for number, first in enumerate(range(0, hidden_units, tile)):
+        columns = slice(first, first + tile)
+        copies[2 + 2 * number].wait()
+        copies[3 + 2 * number].wait()
+        pre_gate = jnp.dot(rows, gate_ref[:, columns], preferred_element_type=jnp.float32)
+        pre_up = jnp.dot(rows, up_ref[:, columns], preferred_element_type=jnp.float32)
+        silu_gate, slope = gate_parts(pre_gate)
+        activation = (silu_gate * pre_up).astype(jnp.bfloat16)
+        slope_ref[:, columns] = slope * pre_up
+        silu_ref[:, columns] = silu_gate
+        act_ref[:, columns] = activation
+        total = jnp.sum(activation.astype(jnp.float32) * low, axis=0, keepdims=True)
+        part_ref[:, columns] = jnp.concatenate([total, jnp.zeros((7, tile), jnp.float32)], axis=0)
+        for start in range(0, model_width, tile):
+            block = slice(start, start + tile)
+            turn_block(gate_ref, gate_turned_ref, block, columns)
+            turn_block(up_ref, up_turned_ref, block, columns)
+    copies[-1].wait()
+    for first in range(0, hidden_units, tile):
+        for start in range(0, model_width, tile):
+            turn_block(
+                down_ref, down_turned_ref, slice(first, first + tile), slice(start, start + tile)
+            )
+
+
+def own_front(side, normed, router_rows, matrices, grades, passage_ranks, earlier=()):
+    model_width, hidden_units = matrices[0].shape
+    token_count = normed.shape[0]
+    ins = [grades, passage_ranks, *matrices, pinned(router_rows), pinned(normed)]
+    return kernel_call(
+        functools.partial(on_side, side, own_kernel, len(earlier), len(ins)),
+        "own",
+        [
+            kept((8, token_count), jnp.float32),
+            kept((token_count, 8), jnp.float32),
+            kept((token_count, hidden_units), jnp.float32),
+            kept((token_count, hidden_units), jnp.float32),
+            kept((token_count, hidden_units), jnp.bfloat16),
+            kept((8, hidden_units), jnp.float32),
+            kept((8, 128), jnp.float32),
+            *(kept(matrix.shape, jnp.bfloat16) for matrix in matrices),
+            *(kept(matrix.shape[::-1], jnp.bfloat16) for matrix in matrices),
+        ],
+        ins,
+        range(5),
+        [
+            pltpu.SMEM(grades.shape, jnp.int32),
+            pltpu.SMEM(grades.shape, jnp.int32),
+            pltpu.SemaphoreType.DMA((3 + 2 * (hidden_units // 256),)),
+        ],
+        earlier=earlier,
     )
 
 
@@ -591,19 +666,7 @@
     return jnp.sum(jnp.sum(values, axis=1, keepdims=True), axis=0, keepdims=True)
 
 
-def pair_kernel(
-    grades_far, ranks_far, down_far, swap_gain_ref, down_ref, grades_ref, ranks_ref, copy_sems
-):
-    down_copy = pltpu.make_async_copy(down_far, down_ref, copy_sems.at[2])
-    down_copy.start()
-    copies = [
-        pltpu.make_async_copy(grades_far, grades_ref, copy_sems.at[0]),
-        pltpu.make_async_copy(ranks_far, ranks_ref, copy_sems.at[1]),
-    ]
-    for copy in copies:
-        copy.start()
-    for copy in copies:
-        copy.wait()
+def swap_gains(grades_ref, ranks_ref):
     passages = grades_ref.shape[1]
     row, lane, pair = pairs_of(passages)
     grade_list = [(number, grades_ref[0, number].astype(jnp.float32)) for number in range(passages)]
@@ -624,10 +687,7 @@
     swap_gain = (
         jnp.abs((worth_row - worth_lane) * (discount_row - discount_lane)) / ideal_gain
     )
-    swap_gain_ref[...] = jnp.where(
-        jnp.logical_and(pair, grade_row > grade_lane), swap_gain, 0.0
-    )
-    down_copy.wait()
+    return jnp.where(jnp.logical_and(pair, grade_row > grade_lane), swap_gain, 0.0)
 
 
 def rank_kernel(swap_gain_ref, near_scores_ref, far_scores_ref, loss_ref, factor_ref):
@@ -754,23 +814,12 @@
         ],
     )
     others = [swap(matrix, CORE) for matrix in mine]
+    arrays = own_front(1, normed, router_rows, mine, grades, passage_ranks)
+    normed, *arrays = lax.optimization_barrier((normed, *arrays))
     x_rows, y_rows = swap(normed, ACROSS_X), swap(normed, ACROSS_Y)
-    turned_gates, own_gates, *own_saved, own_part, mine[0], mine[1] = front(
-        0, (0,), (0,), [normed], router_rows, mine[:2]
-    )
-    swap_gain, mine[2] = kernel_call(
-        pair_kernel,
-        "pairs",
-        [kept((8, 128), jnp.float32), kept(down_matrix.shape, jnp.bfloat16)],
-        [grades, after(passage_ranks, own_part), down_matrix],
-        (0, 1, 2),
-        [
-            pltpu.SMEM(grades.shape, jnp.int32),
-            pltpu.SMEM(grades.shape, jnp.int32),
-            pltpu.SemaphoreType.DMA((3,)),
-        ],
-    )
-    *mine_turned, down_turned = turn(mine)
+    arrays = own_front(0, normed, router_rows, mine, grades, passage_ranks, arrays)
+    turned_gates, own_gates, *own_saved, own_part, swap_gain = arrays[:7]
+    mine, (*mine_turned, down_turned) = list(arrays[7:10]), arrays[10:]
     x_rows, y_rows = after(x_rows, mine_turned[0]), after(y_rows, mine_turned[0])
     far_low = swap(half_of(x_rows, 0), ACROSS_Y)
     far_high = swap(half_of(y_rows, 1), ACROSS_X)
@@ -811,7 +860,7 @@
     )
     matrices = [*mine_turned, *others_turned]
     middle = model_width // 2
-    lower, upper, early, earlier = (0, middle), (middle, model_width), middle + 32, middle + 64
+    lower, upper, early, earlier = (0, middle), (middle, model_width), middle + 32, middle + 48
     far_low, far_high = back(
         ((3, (0, 0), ((0, 0), (1, 0)), (lower, upper), (earlier, earlier)),),
         near, other_near, [far_gates], [far_saved[:3], far_saved[3:]], matrices, token_count,

time: 61.9 us -> 61.3 us (level)
  the two profiles are of different devices: /device:TPU:0 before, /device:TPU:1 now
where the time goes in v2:
time: 61.3 us; the launch traced here: 61.2 us
  Pallas kernels  31.1 us (51%)
  starting transfers between devices  17.3 us (28%)
  waiting for transfers between devices  11.8 us (19%)
  between operations  1 us (2%)
    pallas_call x19, Pallas kernels, kernel_call(): pl.pallas_call(body, name=name, out_shape=outs, in_specs=[pl.BlockSpec(me...  31.1 us
    ppermute x16, starting transfers between devices, swap(): lax.ppermute(value, 'exp', [(index, index ^ bit) for index in range(size)])  13.7 us
    ppermute x16, waiting for transfers between devices, swap(): lax.ppermute(value, 'exp', [(index, index ^ bit) for index in range(size)])  11.8 us
    ppermute x1, starting transfers between devices, every_expert(): lax.ppermute(near_scores, 'psg', [(index, index ^ 2) for index in range(p...  2.31 us
    ppermute x1, starting transfers between devices, every_expert(): lax.ppermute(travelling, 'psg', [(index, index ^ 1) for index in range(pa...  1.3 us
  transfers between devices with their start and end apart: 18, of which 6 were waited for; matrix products, arithmetic and copies ran while one was open for 0% of the time, Pallas kernels for 37%

profile of v2, /device:TPU:1, one launch (start us, length us, event | category | flops | bytes accessed | tf_op | source)
XLA Modules:
  0.0 61.2 jit_solution(428854363843421831)
XLA Ops:
  0.8 0.5 collective-permute-start.3
  1.3 1.4 %norm.1 = (bf16[128,2048]{1,0:T(8,128)(2,1)S(1)}, f32[1,2048]{1,0:T(1,128)S(1)}, bf16[8,2048]{1,0:T(8,128)(2,1)S(1)}, bf16[128,2048]{1,0:T(8,128)(2,1)S(1)}, f32...) custom-call(bf16[128,2048]{1,0:T(8,128)(2,1)} %bitcast.19, f32[1,2048]{1,0:T(1,128)} %bitcast.22, bf16[8,2048]{1,0:T(8,128)(2,1)} %bitcast.21, ...), custom_call_target="tpu_custom_call" | custom-call | flops 1 | bytes 1 | tf_op jit(solution)/shard_map/norm/pallas_call | solution.py:245
  2.7 5.3 %own.2 = (f32[8,128]{1,0:T(8,128)S(1)}, f32[128,8]{1,0:T(8,128)S(1)}, f32[128,768]{1,0:T(8,128)S(1)}, f32[128,768]{1,0:T(8,128)S(1)}, bf16[128,768]{1,0:T(8,128)...) custom-call(s32[1,4]{1,0:T(1,128)} %refs_0_.3, ...), custom_call_target="tpu_custom_call" | custom-call | flops 1 | bytes 1 | tf_op jit(solution)/shard_map/own/pallas_call | solution.py:245
  8.0 2.7 %collective-permute-start.2 = (bf16[128,2048]{1,0:T(8,128)(2,1)S(1)}, bf16[128,2048]{1,0:T(8,128)(2,1)S(1)}, u32[]{:S(2)}, u32[]{:S(2)}) collective-permute-start(bf16[128,2048]{1,0:T(8,128)(2,1)S(1)} %get-tuple-element.117.refs_6_.refs_2_), channel_id=1, source_target_pairs={{0,4},{1,5},{2,6},{3,7},{4,0},{5,1},{6,2},{7,3},{8,12},{9,13},{10,... | collective-permute-start | bytes 1572872 | tf_op jit(solution)/shard_map/ppermute | solution.py:219
  10.8 1.2 %collective-permute-start.1 = (bf16[128,2048]{1,0:T(8,128)(2,1)S(1)}, bf16[128,2048]{1,0:T(8,128)(2,1)S(1)}, u32[]{:S(2)}, u32[]{:S(2)}) collective-permute-start(bf16[128,2048]{1,0:T(8,128)(2,1)S(1)} %get-tuple-element.117.refs_6_.refs_2_), channel_id=1, source_target_pairs={{0,2},{1,3},{2,0},{3,1},{4,6},{5,7},{6,4},{7,5},{8,10},{9,11},{10,... | collective-permute-start | bytes 1572872 | tf_op jit(solution)/shard_map/ppermute | solution.py:219
  12.1 6.2 %collective-permute-done.2.refs_3_.refs_4_.rows_ref = bf16[128,2048]{1,0:T(8,128)(2,1)S(1)} collective-permute-done((bf16[128,2048]{1,0:T(8,128)(2,1)S(1)}, bf16[128,2048]{1,0:T(8,128)(2,1)S(1)}, u32[]{:S(2)}, u32[]{:S(2)}) %collective-permute-start.2) | collective-permute-done | bytes 524320 | tf_op jit(solution)/shard_map/ppermute | solution.py:219
  18.3 1.8 %collective-permute-start.5 = (bf16[64,2048]{1,0:T(8,128)(2,1)S(1)}, bf16[64,2048]{1,0:T(8,128)(2,1)S(1)}, u32[]{:S(2)}, u32[]{:S(2)}) collective-permute-start(bf16[64,2048]{1,0:T(8,128)(2,1)S(1)} %half.3), channel_id=1, source_target_pairs={{0,2},{1,3},{2,0},{3,1},{4,6},{5,7},{6,4},{7,5},{8,10},{9,11},{10,... | collective-permute-start | bytes 786440 | tf_op jit(solution)/shard_map/ppermute | solution.py:219
  20.1 2.8 %collective-permute-done.1.refs_2_.rows_ref.refs_3_ = bf16[128,2048]{1,0:T(8,128)(2,1)S(1)} collective-permute-done((bf16[128,2048]{1,0:T(8,128)(2,1)S(1)}, bf16[128,2048]{1,0:T(8,128)(2,1)S(1)}, u32[]{:S(2)}, u32[]{:S(2)}) %collective-permute-start.1) | collective-permute-done | bytes 524320 | tf_op jit(solution)/shard_map/ppermute | solution.py:219
  22.9 2.1 %front.3 = (f32[256,8]{1,0:T(8,128)S(1)}, f32[256,768]{1,0:T(8,128)S(1)}, f32[256,768]{1,0:T(8,128)S(1)}, bf16[256,768]{1,0:T(8,128)(2,1)S(1)}, f32[8,768]{1,0:T(8,128)S(1)}) custom-call(bf16[8,2048]{1,0:T(8,128)(2,1)S(1)} %get-tuple-element.102.refs_5_.router_ref, bf16[2048,768]{1,0:T(8,128)(2,1)S(1)} %get-tuple-element.132.refs_0_, ...), custom_call_target="tpu_custom_call" | custom-call | flops 1 | bytes 1 | tf_op jit(solution)/shard_map/front/pallas_call | solution.py:245
  25.1 3.4 %front.4 = (f32[384,8]{1,0:T(8,128)}, f32[384,768]{1,0:T(8,128)S(1)}, f32[384,768]{1,0:T(8,128)S(1)}, bf16[384,768]{1,0:T(8,128)(2,1)S(1)}, f32[8,768]{1,0:T(8,128)S(1)}) custom-call(bf16[8,2048]{1,0:T(8,128)(2,1)S(1)} %get-tuple-element.102.refs_5_.router_ref, bf16[2048,768]{1,0:T(8,128)(2,1)S(1)} %collective-permute-done.refs_0_.refs_2_, ...), custom_call_target="tpu_custom_call" | custom-call | flops 1 | bytes 1 | tf_op jit(solution)/shard_map/front/pallas_call | solution.py:245
  28.5 3.0 %front.5 = (f32[128,8]{1,0:T(8,128)S(1)}, f32[128,768]{1,0:T(8,128)S(1)}, f32[128,768]{1,0:T(8,128)S(1)}, bf16[128,768]{1,0:T(8,128)(2,1)S(1)}, f32[128,768]{1,0...) custom-call(bf16[8,2048]{1,0:T(8,128)(2,1)S(1)} %get-tuple-element.102.refs_5_.router_ref, ...), custom_call_target="tpu_custom_call" | custom-call | flops 1 | bytes 1 | tf_op jit(solution)/shard_map/front/pallas_call | solution.py:245
  31.5 1.3 %collective-permute-start.7 = (f32[4,2048]{1,0:T(4,128)S(1)}, f32[4,2048]{1,0:T(4,128)S(1)}, u32[]{:S(2)}, u32[]{:S(2)}) collective-permute-start(f32[4,2048]{1,0:T(4,128)S(1)} %get-tuple-element.145.own_ref), channel_id=1, source_target_pairs={{0,2},{1,3},{2,0},{3,1},{4,6},{5,7},{6,4},{7,5},{8,10},{9,11},{10,... | collective-permute-start | bytes 98312 | tf_op jit(solution)/shard_map/ppermute | solution.py:219
  32.8 1.4 %collective-permute-start.8 = (f32[4,2048]{1,0:T(4,128)S(1)}, f32[4,2048]{1,0:T(4,128)S(1)}, u32[]{:S(2)}, u32[]{:S(2)}) collective-permute-start(f32[4,2048]{1,0:T(4,128)S(1)} %get-tuple-element.145.own_ref), channel_id=1, source_target_pairs={{0,4},{1,5},{2,6},{3,7},{4,0},{5,1},{6,2},{7,3},{8,12},{9,13},{10,... | collective-permute-start | bytes 98312 | tf_op jit(solution)/shard_map/ppermute | solution.py:219
  34.2 2.6 %turn.1 = (bf16[768,2048]{1,0:T(8,128)(2,1)S(1)}, bf16[768,2048]{1,0:T(8,128)(2,1)S(1)}, bf16[2048,768]{1,0:T(8,128)(2,1)S(1)}) custom-call(bf16[2048,768]{1,0:T(8,128)(2,1)S(1)} %collective-permute-done.refs_0_.refs_2_, bf16[2048,768]{1,0:T(8,128)(2,1)S(1)} %collective-permute-done.3.refs_1_.refs_3_, ...), custom_call_target="tpu_custom_call" | custom-call | flops 1 | bytes 1 | tf_op jit(solution)/shard_map/turn/pallas_call | solution.py:245
  36.9 1.0 %collective-permute-done.9.far_ref = f32[4,2048]{1,0:T(4,128)S(1)} collective-permute-done((f32[4,2048]{1,0:T(4,128)S(1)}, f32[4,2048]{1,0:T(4,128)S(1)}, u32[]{:S(2)}, u32[]{:S(2)}) %collective-permute-start.9) | collective-permute-done | bytes 32800 | tf_op jit(solution)/shard_map/ppermute | solution.py:219
  37.9 1.7 %near.1 = (f32[8,768]{1,0:T(8,128)S(1)}, f32[8,768]{1,0:T(8,128)S(1)}, f32[1,2048]{1,0:T(1,128)S(1)}, f32[1,128]{1,0:T(1,128)S(1)}, f32[1,1]{1,0:T(1,128)}) custom-call(f32[4,2048]{1,0:T(4,128)S(1)} %get-tuple-element.145.own_ref, f32[4,2048]{1,0:T(4,128)S(1)} %collective-permute-done.7.x_ref, f32[4,2048]{1,0:T(4,128)S(1)} %collective-permute-done.8.y_ref, ...), custom_call_target="tpu_custom_call" | custom-call | flops 1 | bytes 1 | tf_op jit(solution)/shard_map/near/pallas_call | solution.py:245
  39.6 2.1 %back.4 = (bf16[1072,128]{1,0:T(8,128)(2,1)S(1)}, bf16[1072,128]{1,0:T(8,128)(2,1)S(1)}) custom-call(f32[8,768]{1,0:T(8,128)S(1)} %get-tuple-element.173.near_ref, f32[8,768]{1,0:T(8,128)S(1)} %get-tuple-element.186.other_near_ref, f32[128,8]{1,0:T(8,128)S(1)} %get-tuple-element.154.refs_0_, f32[128,768]{1,0:T(8,128)S(1)} %get-tuple-element.155.refs_1_, ...), custom_call_target="tpu_custom_call" | custom-call | flops 1 | bytes 1 | tf_op jit(solution)/shard_map/back/pallas_call | solution.py:245
  41.7 0.5 collective-permute-start.10
  42.1 1.2 %collective-permute-start.12 = (bf16[1072,128]{1,0:T(8,128)(2,1)S(1)}, bf16[1072,128]{1,0:T(8,128)(2,1)S(1)}, u32[]{:S(2)}, u32[]{:S(2)}) collective-permute-start(bf16[1072,128]{1,0:T(8,128)(2,1)S(1)} %get-tuple-element.163), channel_id=1, source_target_pairs={{0,2},{1,3},{2,0},{3,1},{4,6},{5,7},{6,4},{7,5},{8,10},{9,11},{10,... | collective-permute-start | bytes 823304 | tf_op jit(solution)/shard_map/ppermute | solution.py:219
  43.4 2.4 %back.5 = (bf16[1056,128]{1,0:T(8,128)(2,1)S(1)}, bf16[1056,128]{1,0:T(8,128)(2,1)S(1)}) custom-call(f32[8,768]{1,0:T(8,128)S(1)} %get-tuple-element.173.near_ref, f32[8,768]{1,0:T(8,128)S(1)} %get-tuple-element.186.other_near_ref, f32[256,8]{1,0:T(8,128)S(1)} %get-tuple-element.165.refs_0_, f32[256,768]{1,0:T(8,128)S(1)} %get-tuple-element.166.refs_1_, ...), custom_call_target="tpu_custom_call" | custom-call | flops 1 | bytes 1 | tf_op jit(solution)/shard_map/back/pallas_call | solution.py:245
  46.0 1.1 %collective-permute-start.15 = (bf16[1056,128]{1,0:T(8,128)(2,1)S(1)}, bf16[1056,128]{1,0:T(8,128)(2,1)S(1)}, u32[]{:S(2)}, u32[]{:S(2)}) collective-permute-start(bf16[1056,128]{1,0:T(8,128)(2,1)S(1)} %get-tuple-element.192), channel_id=1, source_target_pairs={{0,4},{1,5},{2,6},{3,7},{4,0},{5,1},{6,2},{7,3},{8,12},{9,13},{10,... | collective-permute-start | bytes 811016 | tf_op jit(solution)/shard_map/ppermute | solution.py:219
  47.1 1.3 %collective-permute-start.11 = (f32[1,128]{1,0:T(1,128)S(1)}, f32[1,128]{1,0:T(1,128)S(1)}, u32[]{:S(2)}, u32[]{:S(2)}) collective-permute-start(f32[1,128]{1,0:T(1,128)S(1)} %get-tuple-element.178.first_ref), channel_id=1, source_target_pairs={{0,8},{8,0},{16,24},{24,16},{1,9},{9,1},{17,25},{25,17},{2,10},{10... | collective-permute-start | bytes 1544 | tf_op jit(solution)/shard_map/ppermute | solution.py:886
  48.4 2.1 %back.6 = (bf16[1040,128]{1,0:T(8,128)(2,1)S(1)}, bf16[1024,128]{1,0:T(8,128)(2,1)S(1)}) custom-call(f32[8,768]{1,0:T(8,128)S(1)} %get-tuple-element.173.near_ref, f32[8,768]{1,0:T(8,128)S(1)} %get-tuple-element.186.other_near_ref, f32[256,8]{1,0:T(8,128)S(1)} %get-tuple-element.165.refs_0_, f32[256,768]{1,0:T(8,128)S(1)} %get-tuple-element.166.refs_1_, ...), custom_call_target="tpu_custom_call" | custom-call | flops 1 | bytes 1 | tf_op jit(solution)/shard_map/back/pallas_call | solution.py:245
  50.9 1.0 %collective-permute-start.16 = (bf16[1040,128]{1,0:T(8,128)(2,1)S(1)}, bf16[1040,128]{1,0:T(8,128)(2,1)S(1)}, u32[]{:S(2)}, u32[]{:S(2)}) collective-permute-start(bf16[1040,128]{1,0:T(8,128)(2,1)S(1)} %get-tuple-element.195), channel_id=1, source_target_pairs={{0,2},{1,3},{2,0},{3,1},{4,6},{5,7},{6,4},{7,5},{8,10},{9,11},{10,... | collective-permute-start | bytes 798728 | tf_op jit(solution)/shard_map/ppermute | solution.py:219
  51.9 0.5 collective-permute-start.17
  52.4 2.3 %collective-permute-start.13 = (f32[2,128]{1,0:T(2,128)S(1)}, f32[2,128]{1,0:T(2,128)S(1)}, u32[]{:S(2)}, u32[]{:S(2)}) collective-permute-start(f32[2,128]{1,0:T(2,128)S(1)} %pack.1.near_scores_ref), channel_id=1, source_target_pairs={{0,16},{8,24},{16,0},{24,8},{1,17},{9,25},{17,1},{25,9},{2,18},{10... | collective-permute-start | bytes 3080 | tf_op jit(solution)/shard_map/ppermute | solution.py:903
  54.7 2.1 %back.7.own_ref = bf16[2064,128]{1,0:T(8,128)(2,1)S(1)} custom-call(f32[8,768]{1,0:T(8,128)S(1)} %get-tuple-element.173.near_ref, f32[8,768]{1,0:T(8,128)S(1)} %get-tuple-element.186.other_near_ref, f32[128,8]{1,0:T(8,128)S(1)} %get-tuple-element.187.refs_0_, f32[128,768]{1,0:T(8,128)S(1)} %get-tuple-element.188.refs_1_, ...), custom_call_target="tpu_custom_call" | custom-call | flops 1 | bytes 1 | tf_op jit(solution)/shard_map/back/pallas_call | solution.py:245
  56.8 0.6 %rank.1 = (f32[1,1]{1,0:T(1,128)}, f32[1,128]{1,0:T(1,128)S(1)}) custom-call(f32[8,128]{1,0:T(8,128)S(1)} %get-tuple-element.131.swap_gain_ref, f32[2,128]{1,0:T(2,128)S(1)} %pack.1.near_scores_ref, f32[2,128]{1,0:T(2,128)S(1)} %collective-permute-done.13.far_scores_ref), custom_call_target="tpu_custom_call" | custom-call | flops 1 | bytes 1 | tf_op jit(solution)/shard_map/rank/pallas_call | solution.py:245
  57.4 0.3 first_end.1
  57.7 0.7 %collective-permute-done.17.y_low_ref = bf16[1024,128]{1,0:T(8,128)(2,1)S(1)} collective-permute-done((bf16[1024,128]{1,0:T(8,128)(2,1)S(1)}, bf16[1024,128]{1,0:T(8,128)(2,1)S(1)}, u32[]{:S(2)}, u32[]{:S(2)}) %collective-permute-start.17) | collective-permute-done | bytes 262176 | tf_op jit(solution)/shard_map/ppermute | solution.py:219
  58.5 0.8 %collective-permute-done.16.x_high_ref = bf16[1040,128]{1,0:T(8,128)(2,1)S(1)} collective-permute-done((bf16[1040,128]{1,0:T(8,128)(2,1)S(1)}, bf16[1040,128]{1,0:T(8,128)(2,1)S(1)}, u32[]{:S(2)}, u32[]{:S(2)}) %collective-permute-start.16) | collective-permute-done | bytes 266272 | tf_op jit(solution)/shard_map/ppermute | solution.py:219
  59.2 1.8 %end.1 = bf16[128,2048]{1,0:T(8,128)(2,1)} custom-call(f32[1,128]{1,0:T(1,128)S(1)} %get-tuple-element.185.factor_ref, f32[128,2048]{1,0:T(8,128)S(1)} %get-tuple-element.193.total_ref, f32[8,128]{1,0:T(8,128)S(1)} %get-tuple-element.194.lines_ref, bf16[1040,128]{1,0:T(8,128)(2,1)S(1)} %collective-permute-done.16.x_high_ref, ...), custom_call_target="tpu_custom_call" | custom-call | flops 1 | bytes 1 | tf_op jit(solution)/shard_map/end/pallas_call | solution.py:245
  (23 shorter events, 1.1 us)
Async XLA Ops:
  0.6 24.4 %collective-permute-start = (bf16[2048,768]{1,0:T(8,128)(2,1)}, bf16[2048,768]{1,0:T(8,128)(2,1)S(1)}, u32[]{:S(2)}, u32[]{:S(2)}) collective-permute-start(bf16[2048,768]{1,0:T(8,128)(2,1)} %bitcast.10), channel_id=1, source_target_pairs={{0,1},{1,0},{2,3},{3,2},{4,5},{5,4},{6,7},{7,6},{8,9},{9,8},{10,11... | collective-permute-start | bytes 9437192 | tf_op jit(solution)/shard_map/ppermute | solution.py:219
  0.8 24.3 %collective-permute-start.3 = (bf16[2048,768]{1,0:T(8,128)(2,1)}, bf16[2048,768]{1,0:T(8,128)(2,1)S(1)}, u32[]{:S(2)}, u32[]{:S(2)}) collective-permute-start(bf16[2048,768]{1,0:T(8,128)(2,1)} %bitcast.13), channel_id=1, source_target_pairs={{0,1},{1,0},{2,3},{3,2},{4,5},{5,4},{6,7},{7,6},{8,9},{9,8},{10,11... | collective-permute-start | bytes 9437192 | tf_op jit(solution)/shard_map/ppermute | solution.py:219
  1.2 27.3 %collective-permute-start.6 = (bf16[768,2048]{1,0:T(8,128)(2,1)}, bf16[768,2048]{1,0:T(8,128)(2,1)S(1)}, u32[]{:S(2)}, u32[]{:S(2)}) collective-permute-start(bf16[768,2048]{1,0:T(8,128)(2,1)} %bitcast.16), channel_id=1, source_target_pairs={{0,1},{1,0},{2,3},{3,2},{4,5},{5,4},{6,7},{7,6},{8,9},{9,8},{10,11... | collective-permute-start | bytes 9437192 | tf_op jit(solution)/shard_map/ppermute | solution.py:219
  8.0 10.2 %collective-permute-start.2 = (bf16[128,2048]{1,0:T(8,128)(2,1)S(1)}, bf16[128,2048]{1,0:T(8,128)(2,1)S(1)}, u32[]{:S(2)}, u32[]{:S(2)}) collective-permute-start(bf16[128,2048]{1,0:T(8,128)(2,1)S(1)} %get-tuple-element.117.refs_6_.refs_2_), channel_id=1, source_target_pairs={{0,4},{1,5},{2,6},{3,7},{4,0},{5,1},{6,2},{7,3},{8,12},{9,13},{10,... | collective-permute-start | bytes 1572872 | tf_op jit(solution)/shard_map/ppermute | solution.py:219
  10.8 12.1 %collective-permute-start.1 = (bf16[128,2048]{1,0:T(8,128)(2,1)S(1)}, bf16[128,2048]{1,0:T(8,128)(2,1)S(1)}, u32[]{:S(2)}, u32[]{:S(2)}) collective-permute-start(bf16[128,2048]{1,0:T(8,128)(2,1)S(1)} %get-tuple-element.117.refs_6_.refs_2_), channel_id=1, source_target_pairs={{0,2},{1,3},{2,0},{3,1},{4,6},{5,7},{6,4},{7,5},{8,10},{9,11},{10,... | collective-permute-start | bytes 1572872 | tf_op jit(solution)/shard_map/ppermute | solution.py:219
  18.3 10.2 %collective-permute-start.5 = (bf16[64,2048]{1,0:T(8,128)(2,1)S(1)}, bf16[64,2048]{1,0:T(8,128)(2,1)S(1)}, u32[]{:S(2)}, u32[]{:S(2)}) collective-permute-start(bf16[64,2048]{1,0:T(8,128)(2,1)S(1)} %half.3), channel_id=1, source_target_pairs={{0,2},{1,3},{2,0},{3,1},{4,6},{5,7},{6,4},{7,5},{8,10},{9,11},{10,... | collective-permute-start | bytes 786440 | tf_op jit(solution)/shard_map/ppermute | solution.py:219
  22.9 5.6 %collective-permute-start.4 = (bf16[64,2048]{1,0:T(8,128)(2,1)S(1)}, bf16[64,2048]{1,0:T(8,128)(2,1)S(1)}, u32[]{:S(2)}, u32[]{:S(2)}) collective-permute-start(bf16[64,2048]{1,0:T(8,128)(2,1)S(1)} %half.2), channel_id=1, source_target_pairs={{0,4},{1,5},{2,6},{3,7},{4,0},{5,1},{6,2},{7,3},{8,12},{9,13},{10,... | collective-permute-start | bytes 786440 | tf_op jit(solution)/shard_map/ppermute | solution.py:219
  31.5 5.4 %collective-permute-start.7 = (f32[4,2048]{1,0:T(4,128)S(1)}, f32[4,2048]{1,0:T(4,128)S(1)}, u32[]{:S(2)}, u32[]{:S(2)}) collective-permute-start(f32[4,2048]{1,0:T(4,128)S(1)} %get-tuple-element.145.own_ref), channel_id=1, source_target_pairs={{0,2},{1,3},{2,0},{3,1},{4,6},{5,7},{6,4},{7,5},{8,10},{9,11},{10,... | collective-permute-start | bytes 98312 | tf_op jit(solution)/shard_map/ppermute | solution.py:219
  32.8 4.1 %collective-permute-start.8 = (f32[4,2048]{1,0:T(4,128)S(1)}, f32[4,2048]{1,0:T(4,128)S(1)}, u32[]{:S(2)}, u32[]{:S(2)}) collective-permute-start(f32[4,2048]{1,0:T(4,128)S(1)} %get-tuple-element.145.own_ref), channel_id=1, source_target_pairs={{0,4},{1,5},{2,6},{3,7},{4,0},{5,1},{6,2},{7,3},{8,12},{9,13},{10,... | collective-permute-start | bytes 98312 | tf_op jit(solution)/shard_map/ppermute | solution.py:219
  34.2 3.7 %collective-permute-start.9 = (f32[4,2048]{1,0:T(4,128)S(1)}, f32[4,2048]{1,0:T(4,128)S(1)}, u32[]{:S(2)}, u32[]{:S(2)}) collective-permute-start(f32[4,2048]{1,0:T(4,128)S(1)} %get-tuple-element.145.own_ref), channel_id=1, source_target_pairs={{0,6},{1,7},{2,4},{3,5},{4,2},{5,3},{6,0},{7,1},{8,14},{9,15},{10,... | collective-permute-start | bytes 98312 | tf_op jit(solution)/shard_map/ppermute | solution.py:219
  41.7 8.8 %collective-permute-start.10 = (bf16[1072,128]{1,0:T(8,128)(2,1)S(1)}, bf16[1072,128]{1,0:T(8,128)(2,1)S(1)}, u32[]{:S(2)}, u32[]{:S(2)}) collective-permute-start(bf16[1072,128]{1,0:T(8,128)(2,1)S(1)} %get-tuple-element.176), channel_id=1, source_target_pairs={{0,4},{1,5},{2,6},{3,7},{4,0},{5,1},{6,2},{7,3},{8,12},{9,13},{10,... | collective-permute-start | bytes 823304 | tf_op jit(solution)/shard_map/ppermute | solution.py:219
  42.1 8.7 %collective-permute-start.12 = (bf16[1072,128]{1,0:T(8,128)(2,1)S(1)}, bf16[1072,128]{1,0:T(8,128)(2,1)S(1)}, u32[]{:S(2)}, u32[]{:S(2)}) collective-permute-start(bf16[1072,128]{1,0:T(8,128)(2,1)S(1)} %get-tuple-element.163), channel_id=1, source_target_pairs={{0,2},{1,3},{2,0},{3,1},{4,6},{5,7},{6,4},{7,5},{8,10},{9,11},{10,... | collective-permute-start | bytes 823304 | tf_op jit(solution)/shard_map/ppermute | solution.py:219
  45.7 11.6 %collective-permute-start.14 = (bf16[1056,128]{1,0:T(8,128)(2,1)S(1)}, bf16[1056,128]{1,0:T(8,128)(2,1)S(1)}, u32[]{:S(2)}, u32[]{:S(2)}) collective-permute-start(bf16[1056,128]{1,0:T(8,128)(2,1)S(1)} %get-tuple-element.172), channel_id=1, source_target_pairs={{0,2},{1,3},{2,0},{3,1},{4,6},{5,7},{6,4},{7,5},{8,10},{9,11},{10,... | collective-permute-start | bytes 811016 | tf_op jit(solution)/shard_map/ppermute | solution.py:219
  46.0 11.4 %collective-permute-start.15 = (bf16[1056,128]{1,0:T(8,128)(2,1)S(1)}, bf16[1056,128]{1,0:T(8,128)(2,1)S(1)}, u32[]{:S(2)}, u32[]{:S(2)}) collective-permute-start(bf16[1056,128]{1,0:T(8,128)(2,1)S(1)} %get-tuple-element.192), channel_id=1, source_target_pairs={{0,4},{1,5},{2,6},{3,7},{4,0},{5,1},{6,2},{7,3},{8,12},{9,13},{10,... | collective-permute-start | bytes 811016 | tf_op jit(solution)/shard_map/ppermute | solution.py:219
  47.1 3.4 %collective-permute-start.11 = (f32[1,128]{1,0:T(1,128)S(1)}, f32[1,128]{1,0:T(1,128)S(1)}, u32[]{:S(2)}, u32[]{:S(2)}) collective-permute-start(f32[1,128]{1,0:T(1,128)S(1)} %get-tuple-element.178.first_ref), channel_id=1, source_target_pairs={{0,8},{8,0},{16,24},{24,16},{1,9},{9,1},{17,25},{25,17},{2,10},{10... | collective-permute-start | bytes 1544 | tf_op jit(solution)/shard_map/ppermute | solution.py:886
  50.9 8.3 %collective-permute-start.16 = (bf16[1040,128]{1,0:T(8,128)(2,1)S(1)}, bf16[1040,128]{1,0:T(8,128)(2,1)S(1)}, u32[]{:S(2)}, u32[]{:S(2)}) collective-permute-start(bf16[1040,128]{1,0:T(8,128)(2,1)S(1)} %get-tuple-element.195), channel_id=1, source_target_pairs={{0,2},{1,3},{2,0},{3,1},{4,6},{5,7},{6,4},{7,5},{8,10},{9,11},{10,... | collective-permute-start | bytes 798728 | tf_op jit(solution)/shard_map/ppermute | solution.py:219
  51.9 6.6 %collective-permute-start.17 = (bf16[1024,128]{1,0:T(8,128)(2,1)S(1)}, bf16[1024,128]{1,0:T(8,128)(2,1)S(1)}, u32[]{:S(2)}, u32[]{:S(2)}) collective-permute-start(bf16[1024,128]{1,0:T(8,128)(2,1)S(1)} %get-tuple-element.196), channel_id=1, source_target_pairs={{0,4},{1,5},{2,6},{3,7},{4,0},{5,1},{6,2},{7,3},{8,12},{9,13},{10,... | collective-permute-start | bytes 786440 | tf_op jit(solution)/shard_map/ppermute | solution.py:219
  52.4 4.4 %collective-permute-start.13 = (f32[2,128]{1,0:T(2,128)S(1)}, f32[2,128]{1,0:T(2,128)S(1)}, u32[]{:S(2)}, u32[]{:S(2)}) collective-permute-start(f32[2,128]{1,0:T(2,128)S(1)} %pack.1.near_scores_ref), channel_id=1, source_target_pairs={{0,16},{8,24},{16,0},{24,8},{1,17},{9,25},{17,1},{25,9},{2,18},{10... | collective-permute-start | bytes 3080 | tf_op jit(solution)/shard_map/ppermute | solution.py:903

commit v3 on v2

--- a/solution.py
+++ b/solution.py
@@ -408,27 +408,19 @@
     )
 
 
-def turn_block(source_ref, target_ref, rows, columns):
-    target_ref[columns, rows] = source_ref[rows, columns].T
-
-
 def own_kernel(
-    grades_far, ranks_far, gate_far, up_far, down_far, router_ref, rows_ref,
-    turned_ref, gates_ref, slope_ref, silu_ref, act_ref, part_ref, swap_gain_ref,
-    gate_ref, up_ref, down_ref, gate_turned_ref, up_turned_ref, down_turned_ref,
-    grades_ref, ranks_ref, copy_sems,
+    gate_far, up_far, router_ref, rows_ref,
+    turned_ref, gates_ref, slope_ref, silu_ref, act_ref, part_ref, gate_ref, up_ref, copy_sems,
 ):
     hidden_units = gate_ref.shape[1]
-    model_width = gate_ref.shape[0]
     tile = 256
-    pairs = [(grades_far, grades_ref), (ranks_far, ranks_ref)]
+    pairs = []
     for first in range(0, hidden_units, tile):
         columns = slice(first, first + tile)
         pairs += [
             (gate_far.at[:, columns], gate_ref.at[:, columns]),
             (up_far.at[:, columns], up_ref.at[:, columns]),
         ]
-    pairs.append((down_far, down_ref))
     copies = [
         pltpu.make_async_copy(source, target, copy_sems.at[index])
         for index, (source, target) in enumerate(pairs)
@@ -450,13 +442,10 @@
         jnp.where(lane == lax.axis_index("exp"), gates, 0.0), axis=1, keepdims=True
     )
     low = own.astype(jnp.bfloat16).astype(jnp.float32)
-    copies[0].wait()
-    copies[1].wait()
-    swap_gain_ref[...] = swap_gains(grades_ref, ranks_ref)
     for number, first in enumerate(range(0, hidden_units, tile)):
         columns = slice(first, first + tile)
-        copies[2 + 2 * number].wait()
-        copies[3 + 2 * number].wait()
+        copies[2 * number].wait()
+        copies[2 * number + 1].wait()
         pre_gate = jnp.dot(rows, gate_ref[:, columns], preferred_element_type=jnp.float32)
         pre_up = jnp.dot(rows, up_ref[:, columns], preferred_element_type=jnp.float32)
         silu_gate, slope = gate_parts(pre_gate)
@@ -466,22 +455,12 @@
         act_ref[:, columns] = activation
         total = jnp.sum(activation.astype(jnp.float32) * low, axis=0, keepdims=True)
         part_ref[:, columns] = jnp.concatenate([total, jnp.zeros((7, tile), jnp.float32)], axis=0)
-        for start in range(0, model_width, tile):
-            block = slice(start, start + tile)
-            turn_block(gate_ref, gate_turned_ref, block, columns)
-            turn_block(up_ref, up_turned_ref, block, columns)
-    copies[-1].wait()
-    for first in range(0, hidden_units, tile):
-        for start in range(0, model_width, tile):
-            turn_block(
-                down_ref, down_turned_ref, slice(first, first + tile), slice(start, start + tile)
-            )
-
-
-def own_front(side, normed, router_rows, matrices, grades, passage_ranks, earlier=()):
-    model_width, hidden_units = matrices[0].shape
+
+
+def own_front(side, normed, router_rows, matrices, earlier=()):
+    hidden_units = matrices[0].shape[1]
     token_count = normed.shape[0]
-    ins = [grades, passage_ranks, *matrices, pinned(router_rows), pinned(normed)]
+    ins = [*matrices, pinned(router_rows), pinned(normed)]
     return kernel_call(
         functools.partial(on_side, side, own_kernel, len(earlier), len(ins)),
         "own",
@@ -492,18 +471,51 @@
             kept((token_count, hidden_units), jnp.float32),
             kept((token_count, hidden_units), jnp.bfloat16),
             kept((8, hidden_units), jnp.float32),
+            *(kept(matrix.shape, jnp.bfloat16) for matrix in matrices),
+        ],
+        ins,
+        range(2),
+        [pltpu.SemaphoreType.DMA((2 * (hidden_units // 256),))],
+        earlier=earlier,
+    )
+
+
+def ready_kernel(
+    grades_far, ranks_far, down_far, gate_ref, up_ref,
+    swap_gain_ref, down_ref, gate_turned_ref, up_turned_ref, down_turned_ref,
+    grades_ref, ranks_ref, copy_sems,
+):
+    pairs = ((grades_far, grades_ref), (ranks_far, ranks_ref), (down_far, down_ref))
+    copies = [
+        pltpu.make_async_copy(source, target, copy_sems.at[index])
+        for index, (source, target) in enumerate(pairs)
+    ]
+    for copy in copies:
+        copy.start()
+    turn_kernel(gate_ref, up_ref, gate_turned_ref, up_turned_ref)
+    copies[0].wait()
+    copies[1].wait()
+    swap_gain_ref[...] = swap_gains(grades_ref, ranks_ref)
+    copies[2].wait()
+    turn_kernel(down_ref, down_turned_ref)
+
+
+def get_ready(grades, passage_ranks, down_matrix, matrices):
+    return kernel_call(
+        ready_kernel,
+        "ready",
+        [
             kept((8, 128), jnp.float32),
-            *(kept(matrix.shape, jnp.bfloat16) for matrix in matrices),
-            *(kept(matrix.shape[::-1], jnp.bfloat16) for matrix in matrices),
-        ],
-        ins,
-        range(5),
+            kept(down_matrix.shape, jnp.bfloat16),
+            *(kept(matrix.shape[::-1], jnp.bfloat16) for matrix in (*matrices, down_matrix)),
+        ],
+        [grades, passage_ranks, down_matrix, *(pinned(matrix) for matrix in matrices)],
+        range(3),
         [
             pltpu.SMEM(grades.shape, jnp.int32),
             pltpu.SMEM(grades.shape, jnp.int32),
-            pltpu.SemaphoreType.DMA((3 + 2 * (hidden_units // 256),)),
-        ],
-        earlier=earlier,
+            pltpu.SemaphoreType.DMA((3,)),
+        ],
     )
 
 
@@ -814,12 +826,15 @@
         ],
     )
     others = [swap(matrix, CORE) for matrix in mine]
-    arrays = own_front(1, normed, router_rows, mine, grades, passage_ranks)
+    arrays = own_front(1, normed, router_rows, mine[:2])
     normed, *arrays = lax.optimization_barrier((normed, *arrays))
     x_rows, y_rows = swap(normed, ACROSS_X), swap(normed, ACROSS_Y)
-    arrays = own_front(0, normed, router_rows, mine, grades, passage_ranks, arrays)
-    turned_gates, own_gates, *own_saved, own_part, swap_gain = arrays[:7]
-    mine, (*mine_turned, down_turned) = list(arrays[7:10]), arrays[10:]
+    arrays = own_front(0, normed, router_rows, mine[:2], arrays)
+    turned_gates, own_gates, *own_saved, own_part = arrays[:6]
+    mine[:2] = arrays[6:]
+    swap_gain, mine[2], *mine_turned, down_turned = get_ready(
+        grades, passage_ranks, down_matrix, mine[:2]
+    )
     x_rows, y_rows = after(x_rows, mine_turned[0]), after(y_rows, mine_turned[0])
     far_low = swap(half_of(x_rows, 0), ACROSS_Y)
     far_high = swap(half_of(y_rows, 1), ACROSS_X)

time: 61.3 us -> 62 us (1.011)
  the two profiles are of different devices: /device:TPU:1 before, /device:TPU:0 now
where the time goes in v3:
time: 62 us; the launch traced here: 61.9 us
  Pallas kernels  32.1 us (52%)
  starting transfers between devices  22.7 us (37%)
  waiting for transfers between devices  6.13 us (10%)
  between operations  0.97 us (2%)
    pallas_call x20, Pallas kernels, kernel_call(): pl.pallas_call(body, name=name, out_shape=outs, in_specs=[pl.BlockSpec(me...  32.1 us
    ppermute x16, starting transfers between devices, swap(): lax.ppermute(value, 'exp', [(index, index ^ bit) for index in range(size)])  18.8 us
    ppermute x16, waiting for transfers between devices, swap(): lax.ppermute(value, 'exp', [(index, index ^ bit) for index in range(size)])  5.94 us
    ppermute x1, starting transfers between devices, every_expert(): lax.ppermute(near_scores, 'psg', [(index, index ^ 2) for index in range(p...  2.59 us
    ppermute x1, starting transfers between devices, every_expert(): lax.ppermute(travelling, 'psg', [(index, index ^ 1) for index in range(pa...  1.29 us
  transfers between devices with their start and end apart: 18, of which 6 were waited for; matrix products, arithmetic and copies ran while one was open for 0% of the time, Pallas kernels for 38%

profile of v3, /device:TPU:0, one launch (start us, length us, event | category | flops | bytes accessed | tf_op | source)
XLA Modules:
  0.0 61.9 jit_solution(17543487382507077554)
XLA Ops:
  0.6 0.5 collective-permute-start
  1.2 0.4 collective-permute-start.6
  1.7 1.4 %norm.1 = (bf16[128,2048]{1,0:T(8,128)(2,1)S(1)}, f32[1,2048]{1,0:T(1,128)S(1)}, bf16[8,2048]{1,0:T(8,128)(2,1)S(1)}, bf16[128,2048]{1,0:T(8,128)(2,1)S(1)}, f32...) custom-call(bf16[128,2048]{1,0:T(8,128)(2,1)} %bitcast.18, f32[1,2048]{1,0:T(1,128)} %bitcast.21, bf16[8,2048]{1,0:T(8,128)(2,1)} %bitcast.20, ...), custom_call_target="tpu_custom_call" | custom-call | flops 1 | bytes 1 | tf_op jit(solution)/shard_map/norm/pallas_call | solution.py:245
  3.1 2.7 %collective-permute-start.2 = (bf16[128,2048]{1,0:T(8,128)(2,1)S(1)}, bf16[128,2048]{1,0:T(8,128)(2,1)S(1)}, u32[]{:S(2)}, u32[]{:S(2)}) collective-permute-start(bf16[128,2048]{1,0:T(8,128)(2,1)S(1)} %get-tuple-element.102.refs_3_.refs_2_), channel_id=1, source_target_pairs={{0,4},{1,5},{2,6},{3,7},{4,0},{5,1},{6,2},{7,3},{8,12},{9,13},{10,... | collective-permute-start | bytes 1572872 | tf_op jit(solution)/shard_map/ppermute | solution.py:219
  5.8 1.5 %collective-permute-start.1 = (bf16[128,2048]{1,0:T(8,128)(2,1)S(1)}, bf16[128,2048]{1,0:T(8,128)(2,1)S(1)}, u32[]{:S(2)}, u32[]{:S(2)}) collective-permute-start(bf16[128,2048]{1,0:T(8,128)(2,1)S(1)} %get-tuple-element.102.refs_3_.refs_2_), channel_id=1, source_target_pairs={{0,2},{1,3},{2,0},{3,1},{4,6},{5,7},{6,4},{7,5},{8,10},{9,11},{10,... | collective-permute-start | bytes 1572872 | tf_op jit(solution)/shard_map/ppermute | solution.py:219
  7.3 3.7 %own.3 = (f32[8,128]{1,0:T(8,128)S(1)}, f32[128,8]{1,0:T(8,128)S(1)}, f32[128,768]{1,0:T(8,128)S(1)}, f32[128,768]{1,0:T(8,128)S(1)}, bf16[128,768]{1,0:T(8,128)...) custom-call(bf16[2048,768]{1,0:T(8,128)(2,1)} %bitcast.12, ...), custom_call_target="tpu_custom_call", output_to_operand_aliasing={{0}: (4, {}), {1}: (5, {}), {2}: (6, {}), {3}: (7, {}), {4}... | custom-call | flops 1 | bytes 1 | tf_op jit(solution)/shard_map/own/pallas_call | solution.py:245
  11.0 2.9 %ready.1 = (f32[8,128]{1,0:T(8,128)S(1)}, bf16[768,2048]{1,0:T(8,128)(2,1)S(1)}, bf16[768,2048]{1,0:T(8,128)(2,1)S(1)}, bf16[768,2048]{1,0:T(8,128)(2,1)S(1)}, bf16[2048,768]{1,0:T(8,128)(2,1)S(1)}) custom-call(s32[1,4]{1,0:T(1,128)} %grades_far.1, s32[1,4]{1,0:T(1,128)} %ranks_far.1, bf16[768,2048]{1,0:T(8,128)(2,1)} %bitcast.17, ...), custom_call_target="tpu_custom_call" | custom-call | flops 1 | bytes 1 | tf_op jit(solution)/shard_map/ready/pallas_call | solution.py:245
  14.0 1.2 %collective-permute-done.2.refs_3_.refs_4_.rows_ref = bf16[128,2048]{1,0:T(8,128)(2,1)S(1)} collective-permute-done((bf16[128,2048]{1,0:T(8,128)(2,1)S(1)}, bf16[128,2048]{1,0:T(8,128)(2,1)S(1)}, u32[]{:S(2)}, u32[]{:S(2)}) %collective-permute-start.2) | collective-permute-done | bytes 524320 | tf_op jit(solution)/shard_map/ppermute | solution.py:219
  15.2 2.3 %collective-permute-start.5 = (bf16[64,2048]{1,0:T(8,128)(2,1)S(1)}, bf16[64,2048]{1,0:T(8,128)(2,1)S(1)}, u32[]{:S(2)}, u32[]{:S(2)}) collective-permute-start(bf16[64,2048]{1,0:T(8,128)(2,1)S(1)} %half.3), channel_id=1, source_target_pairs={{0,2},{1,3},{2,0},{3,1},{4,6},{5,7},{6,4},{7,5},{8,10},{9,11},{10,... | collective-permute-start | bytes 786440 | tf_op jit(solution)/shard_map/ppermute | solution.py:219
  17.8 1.4 %collective-permute-start.4 = (bf16[64,2048]{1,0:T(8,128)(2,1)S(1)}, bf16[64,2048]{1,0:T(8,128)(2,1)S(1)}, u32[]{:S(2)}, u32[]{:S(2)}) collective-permute-start(bf16[64,2048]{1,0:T(8,128)(2,1)S(1)} %half.2), channel_id=1, source_target_pairs={{0,4},{1,5},{2,6},{3,7},{4,0},{5,1},{6,2},{7,3},{8,12},{9,13},{10,... | collective-permute-start | bytes 786440 | tf_op jit(solution)/shard_map/ppermute | solution.py:219
  19.1 2.1 %front.3 = (f32[256,8]{1,0:T(8,128)S(1)}, f32[256,768]{1,0:T(8,128)S(1)}, f32[256,768]{1,0:T(8,128)S(1)}, bf16[256,768]{1,0:T(8,128)(2,1)S(1)}, f32[8,768]{1,0:T(8,128)S(1)}) custom-call(bf16[8,2048]{1,0:T(8,128)(2,1)S(1)} %get-tuple-element.92.refs_2_.router_ref, bf16[2048,768]{1,0:T(8,128)(2,1)S(1)} %get-tuple-element.111.gate_ref.refs_0_, ...), custom_call_target="tpu_custom_call" | custom-call | flops 1 | bytes 1 | tf_op jit(solution)/shard_map/front/pallas_call | solution.py:245
  21.3 3.4 %front.4 = (f32[384,8]{1,0:T(8,128)}, f32[384,768]{1,0:T(8,128)S(1)}, f32[384,768]{1,0:T(8,128)S(1)}, bf16[384,768]{1,0:T(8,128)(2,1)S(1)}, f32[8,768]{1,0:T(8,128)S(1)}) custom-call(bf16[8,2048]{1,0:T(8,128)(2,1)S(1)} %get-tuple-element.92.refs_2_.router_ref, bf16[2048,768]{1,0:T(8,128)(2,1)S(1)} %collective-permute-done.refs_0_.refs_2_, ...), custom_call_target="tpu_custom_call" | custom-call | flops 1 | bytes 1 | tf_op jit(solution)/shard_map/front/pallas_call | solution.py:245
  24.8 3.0 %front.5 = (f32[128,8]{1,0:T(8,128)S(1)}, f32[128,768]{1,0:T(8,128)S(1)}, f32[128,768]{1,0:T(8,128)S(1)}, bf16[128,768]{1,0:T(8,128)(2,1)S(1)}, f32[128,768]{1,0...) custom-call(bf16[8,2048]{1,0:T(8,128)(2,1)S(1)} %get-tuple-element.92.refs_2_.router_ref,, ...), custom_call_target="tpu_custom_call" | custom-call | flops 1 | bytes 1 | tf_op jit(solution)/shard_map/front/pallas_call | solution.py:245
  27.7 1.6 %collective-permute-start.9 = (f32[4,2048]{1,0:T(4,128)S(1)}, f32[4,2048]{1,0:T(4,128)S(1)}, u32[]{:S(2)}, u32[]{:S(2)}) collective-permute-start(f32[4,2048]{1,0:T(4,128)S(1)} %get-tuple-element.125.own_ref), channel_id=1, source_target_pairs={{0,6},{1,7},{2,4},{3,5},{4,2},{5,3},{6,0},{7,1},{8,14},{9,15},{10,... | collective-permute-start | bytes 98312 | tf_op jit(solution)/shard_map/ppermute | solution.py:219
  29.4 1.8 %collective-permute-start.8 = (f32[4,2048]{1,0:T(4,128)S(1)}, f32[4,2048]{1,0:T(4,128)S(1)}, u32[]{:S(2)}, u32[]{:S(2)}) collective-permute-start(f32[4,2048]{1,0:T(4,128)S(1)} %get-tuple-element.125.own_ref), channel_id=1, source_target_pairs={{0,4},{1,5},{2,6},{3,7},{4,0},{5,1},{6,2},{7,3},{8,12},{9,13},{10,... | collective-permute-start | bytes 98312 | tf_op jit(solution)/shard_map/ppermute | solution.py:219
  31.3 2.6 %turn.1 = (bf16[768,2048]{1,0:T(8,128)(2,1)S(1)}, bf16[768,2048]{1,0:T(8,128)(2,1)S(1)}, bf16[2048,768]{1,0:T(8,128)(2,1)S(1)}) custom-call(bf16[2048,768]{1,0:T(8,128)(2,1)S(1)} %collective-permute-done.refs_0_.refs_2_, bf16[2048,768]{1,0:T(8,128)(2,1)S(1)} %collective-permute-done.3.refs_1_.refs_3_, ...), custom_call_target="tpu_custom_call" | custom-call | flops 1 | bytes 1 | tf_op jit(solution)/shard_map/turn/pallas_call | solution.py:245
  34.0 1.4 %collective-permute-done.7.x_ref = f32[4,2048]{1,0:T(4,128)S(1)} collective-permute-done((f32[4,2048]{1,0:T(4,128)S(1)}, f32[4,2048]{1,0:T(4,128)S(1)}, u32[]{:S(2)}, u32[]{:S(2)}) %collective-permute-start.7) | collective-permute-done | bytes 32800 | tf_op jit(solution)/shard_map/ppermute | solution.py:219
  35.4 1.7 %near.1 = (f32[8,768]{1,0:T(8,128)S(1)}, f32[8,768]{1,0:T(8,128)S(1)}, f32[1,2048]{1,0:T(1,128)S(1)}, f32[1,128]{1,0:T(1,128)S(1)}, f32[1,1]{1,0:T(1,128)}) custom-call(f32[4,2048]{1,0:T(4,128)S(1)} %get-tuple-element.125.own_ref, f32[4,2048]{1,0:T(4,128)S(1)} %collective-permute-done.7.x_ref, f32[4,2048]{1,0:T(4,128)S(1)} %collective-permute-done.8.y_ref, ...), custom_call_target="tpu_custom_call" | custom-call | flops 1 | bytes 1 | tf_op jit(solution)/shard_map/near/pallas_call | solution.py:245
  37.1 2.1 %back.4 = (bf16[1072,128]{1,0:T(8,128)(2,1)S(1)}, bf16[1072,128]{1,0:T(8,128)(2,1)S(1)}) custom-call(f32[8,768]{1,0:T(8,128)S(1)} %get-tuple-element.153.near_ref, f32[8,768]{1,0:T(8,128)S(1)} %get-tuple-element.166.other_near_ref, f32[128,8]{1,0:T(8,128)S(1)} %get-tuple-element.134.refs_0_, f32[128,768]{1,0:T(8,128)S(1)} %get-tuple-element.135.refs_1_, ...), custom_call_target="tpu_custom_call" | custom-call | flops 1 | bytes 1 | tf_op jit(solution)/shard_map/back/pallas_call | solution.py:245
  39.5 0.8 %collective-permute-start.12 = (bf16[1072,128]{1,0:T(8,128)(2,1)S(1)}, bf16[1072,128]{1,0:T(8,128)(2,1)S(1)}, u32[]{:S(2)}, u32[]{:S(2)}) collective-permute-start(bf16[1072,128]{1,0:T(8,128)(2,1)S(1)} %get-tuple-element.143), channel_id=1, source_target_pairs={{0,2},{1,3},{2,0},{3,1},{4,6},{5,7},{6,4},{7,5},{8,10},{9,11},{10,... | collective-permute-start | bytes 823304 | tf_op jit(solution)/shard_map/ppermute | solution.py:219
  40.4 2.1 %back.5 = (bf16[1056,128]{1,0:T(8,128)(2,1)S(1)}, bf16[1056,128]{1,0:T(8,128)(2,1)S(1)}) custom-call(f32[8,768]{1,0:T(8,128)S(1)} %get-tuple-element.153.near_ref, f32[8,768]{1,0:T(8,128)S(1)} %get-tuple-element.166.other_near_ref, f32[256,8]{1,0:T(8,128)S(1)} %get-tuple-element.145.refs_0_, f32[256,768]{1,0:T(8,128)S(1)} %get-tuple-element.146.refs_1_, ...), custom_call_target="tpu_custom_call" | custom-call | flops 1 | bytes 1 | tf_op jit(solution)/shard_map/back/pallas_call | solution.py:245
  42.5 1.2 %collective-permute-start.14 = (bf16[1056,128]{1,0:T(8,128)(2,1)S(1)}, bf16[1056,128]{1,0:T(8,128)(2,1)S(1)}, u32[]{:S(2)}, u32[]{:S(2)}) collective-permute-start(bf16[1056,128]{1,0:T(8,128)(2,1)S(1)} %get-tuple-element.152), channel_id=1, source_target_pairs={{0,2},{1,3},{2,0},{3,1},{4,6},{5,7},{6,4},{7,5},{8,10},{9,11},{10,... | collective-permute-start | bytes 811016 | tf_op jit(solution)/shard_map/ppermute | solution.py:219
  43.7 1.7 %collective-permute-start.15 = (bf16[1056,128]{1,0:T(8,128)(2,1)S(1)}, bf16[1056,128]{1,0:T(8,128)(2,1)S(1)}, u32[]{:S(2)}, u32[]{:S(2)}) collective-permute-start(bf16[1056,128]{1,0:T(8,128)(2,1)S(1)} %get-tuple-element.172), channel_id=1, source_target_pairs={{0,4},{1,5},{2,6},{3,7},{4,0},{5,1},{6,2},{7,3},{8,12},{9,13},{10,... | collective-permute-start | bytes 811016 | tf_op jit(solution)/shard_map/ppermute | solution.py:219
  45.5 1.3 %collective-permute-start.11 = (f32[1,128]{1,0:T(1,128)S(1)}, f32[1,128]{1,0:T(1,128)S(1)}, u32[]{:S(2)}, u32[]{:S(2)}) collective-permute-start(f32[1,128]{1,0:T(1,128)S(1)} %get-tuple-element.158.first_ref), channel_id=1, source_target_pairs={{0,8},{8,0},{16,24},{24,16},{1,9},{9,1},{17,25},{25,17},{2,10},{10... | collective-permute-start | bytes 1544 | tf_op jit(solution)/shard_map/ppermute | solution.py:901
  46.8 2.1 %back.6 = (bf16[1040,128]{1,0:T(8,128)(2,1)S(1)}, bf16[1024,128]{1,0:T(8,128)(2,1)S(1)}) custom-call(f32[8,768]{1,0:T(8,128)S(1)} %get-tuple-element.153.near_ref, f32[8,768]{1,0:T(8,128)S(1)} %get-tuple-element.166.other_near_ref, f32[256,8]{1,0:T(8,128)S(1)} %get-tuple-element.145.refs_0_, f32[256,768]{1,0:T(8,128)S(1)} %get-tuple-element.146.refs_1_, ...), custom_call_target="tpu_custom_call" | custom-call | flops 1 | bytes 1 | tf_op jit(solution)/shard_map/back/pallas_call | solution.py:245
  49.2 0.7 %collective-permute-start.16 = (bf16[1040,128]{1,0:T(8,128)(2,1)S(1)}, bf16[1040,128]{1,0:T(8,128)(2,1)S(1)}, u32[]{:S(2)}, u32[]{:S(2)}) collective-permute-start(bf16[1040,128]{1,0:T(8,128)(2,1)S(1)} %get-tuple-element.175), channel_id=1, source_target_pairs={{0,2},{1,3},{2,0},{3,1},{4,6},{5,7},{6,4},{7,5},{8,10},{9,11},{10,... | collective-permute-start | bytes 798728 | tf_op jit(solution)/shard_map/ppermute | solution.py:219
  49.9 1.4 %collective-permute-start.17 = (bf16[1024,128]{1,0:T(8,128)(2,1)S(1)}, bf16[1024,128]{1,0:T(8,128)(2,1)S(1)}, u32[]{:S(2)}, u32[]{:S(2)}) collective-permute-start(bf16[1024,128]{1,0:T(8,128)(2,1)S(1)} %get-tuple-element.176), channel_id=1, source_target_pairs={{0,4},{1,5},{2,6},{3,7},{4,0},{5,1},{6,2},{7,3},{8,12},{9,13},{10,... | collective-permute-start | bytes 786440 | tf_op jit(solution)/shard_map/ppermute | solution.py:219
  51.3 2.6 %collective-permute-start.13 = (f32[2,128]{1,0:T(2,128)S(1)}, f32[2,128]{1,0:T(2,128)S(1)}, u32[]{:S(2)}, u32[]{:S(2)}) collective-permute-start(f32[2,128]{1,0:T(2,128)S(1)} %pack.1.near_scores_ref), channel_id=1, source_target_pairs={{0,16},{8,24},{16,0},{24,8},{1,17},{9,25},{17,1},{25,9},{2,18},{10... | collective-permute-start | bytes 3080 | tf_op jit(solution)/shard_map/ppermute | solution.py:918
  53.9 2.1 %back.7.own_ref = bf16[2064,128]{1,0:T(8,128)(2,1)S(1)} custom-call(f32[8,768]{1,0:T(8,128)S(1)} %get-tuple-element.153.near_ref, f32[8,768]{1,0:T(8,128)S(1)} %get-tuple-element.166.other_near_ref, f32[128,8]{1,0:T(8,128)S(1)} %get-tuple-element.167.refs_0_, f32[128,768]{1,0:T(8,128)S(1)} %get-tuple-element.168.refs_1_, ...), custom_call_target="tpu_custom_call" | custom-call | flops 1 | bytes 1 | tf_op jit(solution)/shard_map/back/pallas_call | solution.py:245
  56.0 0.6 %rank.1 = (f32[1,1]{1,0:T(1,128)}, f32[1,128]{1,0:T(1,128)S(1)}) custom-call(f32[8,128]{1,0:T(8,128)S(1)} %get-tuple-element.113.swap_gain_ref, f32[2,128]{1,0:T(2,128)S(1)} %pack.1.near_scores_ref, f32[2,128]{1,0:T(2,128)S(1)} %collective-permute-done.13.far_scores_ref), custom_call_target="tpu_custom_call" | custom-call | flops 1 | bytes 1 | tf_op jit(solution)/shard_map/rank/pallas_call | solution.py:245
  57.0 3.0 %collective-permute-done.17.y_low_ref = bf16[1024,128]{1,0:T(8,128)(2,1)S(1)} collective-permute-done((bf16[1024,128]{1,0:T(8,128)(2,1)S(1)}, bf16[1024,128]{1,0:T(8,128)(2,1)S(1)}, u32[]{:S(2)}, u32[]{:S(2)}) %collective-permute-start.17) | collective-permute-done | bytes 262176 | tf_op jit(solution)/shard_map/ppermute | solution.py:219
  60.0 1.7 %end.1 = bf16[128,2048]{1,0:T(8,128)(2,1)} custom-call(f32[1,128]{1,0:T(1,128)S(1)} %get-tuple-element.165.factor_ref, f32[128,2048]{1,0:T(8,128)S(1)} %get-tuple-element.173.total_ref, f32[8,128]{1,0:T(8,128)S(1)} %get-tuple-element.174.lines_ref, bf16[1040,128]{1,0:T(8,128)(2,1)S(1)} %collective-permute-done.16.x_high_ref, ...), custom_call_target="tpu_custom_call" | custom-call | flops 1 | bytes 1 | tf_op jit(solution)/shard_map/end/pallas_call | solution.py:245
  (24 shorter events, 1.6 us)
Async XLA Ops:
  0.6 20.6 %collective-permute-start = (bf16[2048,768]{1,0:T(8,128)(2,1)}, bf16[2048,768]{1,0:T(8,128)(2,1)S(1)}, u32[]{:S(2)}, u32[]{:S(2)}) collective-permute-start(bf16[2048,768]{1,0:T(8,128)(2,1)} %bitcast.10), channel_id=1, source_target_pairs={{0,1},{1,0},{2,3},{3,2},{4,5},{5,4},{6,7},{7,6},{8,9},{9,8},{10,11... | collective-permute-start | bytes 9437192 | tf_op jit(solution)/shard_map/ppermute | solution.py:219
  1.1 20.1 %collective-permute-start.3 = (bf16[2048,768]{1,0:T(8,128)(2,1)}, bf16[2048,768]{1,0:T(8,128)(2,1)S(1)}, u32[]{:S(2)}, u32[]{:S(2)}) collective-permute-start(bf16[2048,768]{1,0:T(8,128)(2,1)} %bitcast.13), channel_id=1, source_target_pairs={{0,1},{1,0},{2,3},{3,2},{4,5},{5,4},{6,7},{7,6},{8,9},{9,8},{10,11... | collective-permute-start | bytes 9437192 | tf_op jit(solution)/shard_map/ppermute | solution.py:219
  1.2 23.5 %collective-permute-start.6 = (bf16[768,2048]{1,0:T(8,128)(2,1)}, bf16[768,2048]{1,0:T(8,128)(2,1)S(1)}, u32[]{:S(2)}, u32[]{:S(2)}) collective-permute-start(bf16[768,2048]{1,0:T(8,128)(2,1)} %bitcast.16), channel_id=1, source_target_pairs={{0,1},{1,0},{2,3},{3,2},{4,5},{5,4},{6,7},{7,6},{8,9},{9,8},{10,11... | collective-permute-start | bytes 9437192 | tf_op jit(solution)/shard_map/ppermute | solution.py:219
  3.1 12.0 %collective-permute-start.2 = (bf16[128,2048]{1,0:T(8,128)(2,1)S(1)}, bf16[128,2048]{1,0:T(8,128)(2,1)S(1)}, u32[]{:S(2)}, u32[]{:S(2)}) collective-permute-start(bf16[128,2048]{1,0:T(8,128)(2,1)S(1)} %get-tuple-element.102.refs_3_.refs_2_), channel_id=1, source_target_pairs={{0,4},{1,5},{2,6},{3,7},{4,0},{5,1},{6,2},{7,3},{8,12},{9,13},{10,... | collective-permute-start | bytes 1572872 | tf_op jit(solution)/shard_map/ppermute | solution.py:219
  5.8 11.9 %collective-permute-start.1 = (bf16[128,2048]{1,0:T(8,128)(2,1)S(1)}, bf16[128,2048]{1,0:T(8,128)(2,1)S(1)}, u32[]{:S(2)}, u32[]{:S(2)}) collective-permute-start(bf16[128,2048]{1,0:T(8,128)(2,1)S(1)} %get-tuple-element.102.refs_3_.refs_2_), channel_id=1, source_target_pairs={{0,2},{1,3},{2,0},{3,1},{4,6},{5,7},{6,4},{7,5},{8,10},{9,11},{10,... | collective-permute-start | bytes 1572872 | tf_op jit(solution)/shard_map/ppermute | solution.py:219
  15.2 9.6 %collective-permute-start.5 = (bf16[64,2048]{1,0:T(8,128)(2,1)S(1)}, bf16[64,2048]{1,0:T(8,128)(2,1)S(1)}, u32[]{:S(2)}, u32[]{:S(2)}) collective-permute-start(bf16[64,2048]{1,0:T(8,128)(2,1)S(1)} %half.3), channel_id=1, source_target_pairs={{0,2},{1,3},{2,0},{3,1},{4,6},{5,7},{6,4},{7,5},{8,10},{9,11},{10,... | collective-permute-start | bytes 786440 | tf_op jit(solution)/shard_map/ppermute | solution.py:219
  17.8 7.0 %collective-permute-start.4 = (bf16[64,2048]{1,0:T(8,128)(2,1)S(1)}, bf16[64,2048]{1,0:T(8,128)(2,1)S(1)}, u32[]{:S(2)}, u32[]{:S(2)}) collective-permute-start(bf16[64,2048]{1,0:T(8,128)(2,1)S(1)} %half.2), channel_id=1, source_target_pairs={{0,4},{1,5},{2,6},{3,7},{4,0},{5,1},{6,2},{7,3},{8,12},{9,13},{10,... | collective-permute-start | bytes 786440 | tf_op jit(solution)/shard_map/ppermute | solution.py:219
  27.7 6.2 %collective-permute-start.9 = (f32[4,2048]{1,0:T(4,128)S(1)}, f32[4,2048]{1,0:T(4,128)S(1)}, u32[]{:S(2)}, u32[]{:S(2)}) collective-permute-start(f32[4,2048]{1,0:T(4,128)S(1)} %get-tuple-element.125.own_ref), channel_id=1, source_target_pairs={{0,6},{1,7},{2,4},{3,5},{4,2},{5,3},{6,0},{7,1},{8,14},{9,15},{10,... | collective-permute-start | bytes 98312 | tf_op jit(solution)/shard_map/ppermute | solution.py:219
  29.4 4.6 %collective-permute-start.8 = (f32[4,2048]{1,0:T(4,128)S(1)}, f32[4,2048]{1,0:T(4,128)S(1)}, u32[]{:S(2)}, u32[]{:S(2)}) collective-permute-start(f32[4,2048]{1,0:T(4,128)S(1)} %get-tuple-element.125.own_ref), channel_id=1, source_target_pairs={{0,4},{1,5},{2,6},{3,7},{4,0},{5,1},{6,2},{7,3},{8,12},{9,13},{10,... | collective-permute-start | bytes 98312 | tf_op jit(solution)/shard_map/ppermute | solution.py:219
  31.2 4.2 %collective-permute-start.7 = (f32[4,2048]{1,0:T(4,128)S(1)}, f32[4,2048]{1,0:T(4,128)S(1)}, u32[]{:S(2)}, u32[]{:S(2)}) collective-permute-start(f32[4,2048]{1,0:T(4,128)S(1)} %get-tuple-element.125.own_ref), channel_id=1, source_target_pairs={{0,2},{1,3},{2,0},{3,1},{4,6},{5,7},{6,4},{7,5},{8,10},{9,11},{10,... | collective-permute-start | bytes 98312 | tf_op jit(solution)/shard_map/ppermute | solution.py:219
  39.2 9.9 %collective-permute-start.10 = (bf16[1072,128]{1,0:T(8,128)(2,1)S(1)}, bf16[1072,128]{1,0:T(8,128)(2,1)S(1)}, u32[]{:S(2)}, u32[]{:S(2)}) collective-permute-start(bf16[1072,128]{1,0:T(8,128)(2,1)S(1)} %get-tuple-element.156), channel_id=1, source_target_pairs={{0,4},{1,5},{2,6},{3,7},{4,0},{5,1},{6,2},{7,3},{8,12},{9,13},{10,... | collective-permute-start | bytes 823304 | tf_op jit(solution)/shard_map/ppermute | solution.py:219
  39.5 9.5 %collective-permute-start.12 = (bf16[1072,128]{1,0:T(8,128)(2,1)S(1)}, bf16[1072,128]{1,0:T(8,128)(2,1)S(1)}, u32[]{:S(2)}, u32[]{:S(2)}) collective-permute-start(bf16[1072,128]{1,0:T(8,128)(2,1)S(1)} %get-tuple-element.143), channel_id=1, source_target_pairs={{0,2},{1,3},{2,0},{3,1},{4,6},{5,7},{6,4},{7,5},{8,10},{9,11},{10,... | collective-permute-start | bytes 823304 | tf_op jit(solution)/shard_map/ppermute | solution.py:219
  42.5 14.1 %collective-permute-start.14 = (bf16[1056,128]{1,0:T(8,128)(2,1)S(1)}, bf16[1056,128]{1,0:T(8,128)(2,1)S(1)}, u32[]{:S(2)}, u32[]{:S(2)}) collective-permute-start(bf16[1056,128]{1,0:T(8,128)(2,1)S(1)} %get-tuple-element.152), channel_id=1, source_target_pairs={{0,2},{1,3},{2,0},{3,1},{4,6},{5,7},{6,4},{7,5},{8,10},{9,11},{10,... | collective-permute-start | bytes 811016 | tf_op jit(solution)/shard_map/ppermute | solution.py:219
  43.7 12.9 %collective-permute-start.15 = (bf16[1056,128]{1,0:T(8,128)(2,1)S(1)}, bf16[1056,128]{1,0:T(8,128)(2,1)S(1)}, u32[]{:S(2)}, u32[]{:S(2)}) collective-permute-start(bf16[1056,128]{1,0:T(8,128)(2,1)S(1)} %get-tuple-element.172), channel_id=1, source_target_pairs={{0,4},{1,5},{2,6},{3,7},{4,0},{5,1},{6,2},{7,3},{8,12},{9,13},{10,... | collective-permute-start | bytes 811016 | tf_op jit(solution)/shard_map/ppermute | solution.py:219
  45.5 3.5 %collective-permute-start.11 = (f32[1,128]{1,0:T(1,128)S(1)}, f32[1,128]{1,0:T(1,128)S(1)}, u32[]{:S(2)}, u32[]{:S(2)}) collective-permute-start(f32[1,128]{1,0:T(1,128)S(1)} %get-tuple-element.158.first_ref), channel_id=1, source_target_pairs={{0,8},{8,0},{16,24},{24,16},{1,9},{9,1},{17,25},{25,17},{2,10},{10... | collective-permute-start | bytes 1544 | tf_op jit(solution)/shard_map/ppermute | solution.py:901
  49.2 10.8 %collective-permute-start.16 = (bf16[1040,128]{1,0:T(8,128)(2,1)S(1)}, bf16[1040,128]{1,0:T(8,128)(2,1)S(1)}, u32[]{:S(2)}, u32[]{:S(2)}) collective-permute-start(bf16[1040,128]{1,0:T(8,128)(2,1)S(1)} %get-tuple-element.175), channel_id=1, source_target_pairs={{0,2},{1,3},{2,0},{3,1},{4,6},{5,7},{6,4},{7,5},{8,10},{9,11},{10,... | collective-permute-start | bytes 798728 | tf_op jit(solution)/shard_map/ppermute | solution.py:219
  49.9 10.1 %collective-permute-start.17 = (bf16[1024,128]{1,0:T(8,128)(2,1)S(1)}, bf16[1024,128]{1,0:T(8,128)(2,1)S(1)}, u32[]{:S(2)}, u32[]{:S(2)}) collective-permute-start(bf16[1024,128]{1,0:T(8,128)(2,1)S(1)} %get-tuple-element.176), channel_id=1, source_target_pairs={{0,4},{1,5},{2,6},{3,7},{4,0},{5,1},{6,2},{7,3},{8,12},{9,13},{10,... | collective-permute-start | bytes 786440 | tf_op jit(solution)/shard_map/ppermute | solution.py:219
  51.3 4.7 %collective-permute-start.13 = (f32[2,128]{1,0:T(2,128)S(1)}, f32[2,128]{1,0:T(2,128)S(1)}, u32[]{:S(2)}, u32[]{:S(2)}) collective-permute-start(f32[2,128]{1,0:T(2,128)S(1)} %pack.1.near_scores_ref), channel_id=1, source_target_pairs={{0,16},{8,24},{16,0},{24,8},{1,17},{9,25},{17,1},{25,9},{2,18},{10... | collective-permute-start | bytes 3080 | tf_op jit(solution)/shard_map/ppermute | solution.py:918
